TPU v7x, 256 devices: a whole 4x4x8 slice. The times are simulated.
256 devices in a mesh: pair: 128 (over z, x, y), aux: 2 (over core).
Axes of the slice: x: 4, y: 4, z: 8, core: 2. Of those that a mesh axis runs over, the one named last changes fastest.
Arguments:
- half_transformed: bfloat16 [256, 128, 32, 128], P('pair', None, 'aux'), may hold values from -1.5 to 1.5
- trials: bfloat16 [256, 128, 128], P('pair'), may hold values from -0.047851562 to 0.047851562
- pair_table: int32 [8192, 2], P('pair'), may hold values from 0 to 255, as said below
- block_slot: int32 [256], replicated, may hold values from 0 to 255, as said below
- domains: int32 [256, 128], replicated, may hold values from 0 to 4591, as said below
Outputs:
- applied: float32 [256, 128, 128], P('pair')
Inputs may be any that keep to these rules, and one draw needn't show every extreme that they name: `block_slot`: A permutation of the block numbers. `pair_table`: both blocks of every pair listed in rows p * 64 to (p + 1) * 64 - 1 stand, by block_slot, in rows (p - 2) * 2 to (p + 3) * 2 - 1 of the blocked arrays. A pair may repeat and may name one block twice. `domains`: the 128 orbital numbers of one row are distinct.
All inputs are finite; a program needn't handle non-finite values.
Results may differ from a plain program's by a relative error of at most 0.0022.
Values may be sent and summed in bfloat16 or wider, within the bound.
A program may use at most 64 MiB of HBM per device.

v0:
```python
import jax
import jax.numpy as jnp
from jax import lax
from jax.sharding import PartitionSpec as P

BS = 128
REACH = 2


pair_group = 8


def shifted(shard, axis, by):
    count = lax.axis_size(axis)
    pairs = [(i, i + by) for i in range(count) if 0 <= i + by < count]
    return lax.ppermute(shard, axis, pairs)


def local(half_transformed, trials, pair_table, block_slot, domains):
    blocks_here = half_transformed.shape[0]
    aux_width = half_transformed.shape[2]
    orbital_width = half_transformed.shape[3]
    vector_width = trials.shape[2]
    pair_rows = pair_table.shape[0]
    my_index = lax.axis_index("pair")
    packed = jnp.concatenate(
        [half_transformed.reshape(blocks_here, BS, aux_width * orbital_width), trials], axis=2
    )
    received = {0: packed}
    for offset in range(-REACH, REACH + 1):
        if offset != 0:
            received[offset] = shifted(packed, "pair", -offset)
    window = jnp.concatenate([received[offset] for offset in range(-REACH, REACH + 1)], axis=0)
    near_count = window.shape[0]
    near_blocks = window[:, :, : aux_width * orbital_width].reshape(
        near_count, BS, aux_width, orbital_width
    )
    near_trials = window[:, :, aux_width * orbital_width :]
    block_count = block_slot.shape[0]
    numbers = lax.broadcasted_iota(jnp.int32, (1, 1, block_count), 2)
    pair_slots = jnp.sum(
        jnp.where(pair_table[:, :, None] == numbers, block_slot[None, None, :], 0), axis=2
    )
    near_index = (
        pair_slots // blocks_here - my_index + REACH
    ) * blocks_here + pair_slots % blocks_here
    pair_domains = jnp.take(domains, pair_table, axis=0)
    keep_right = (pair_table[:, 0] != pair_table[:, 1]).astype(jnp.float32)

    def group_step(group_index, partial_value):
        first_row = group_index * pair_group
        index_a = lax.dynamic_slice_in_dim(near_index[:, 0], first_row, pair_group)
        index_b = lax.dynamic_slice_in_dim(near_index[:, 1], first_row, pair_group)
        domain_a = lax.dynamic_slice_in_dim(pair_domains[:, 0], first_row, pair_group)
        domain_b = lax.dynamic_slice_in_dim(pair_domains[:, 1], first_row, pair_group)
        keep = lax.dynamic_slice_in_dim(keep_right, first_row, pair_group)
        left_block = jnp.take(near_blocks, index_a, axis=0)
        right_block = jnp.take(near_blocks, index_b, axis=0)
        left_vec = jnp.take(near_trials, index_a, axis=0)
        right_vec = jnp.take(near_trials, index_b, axis=0)
        intersection = (domain_a[:, :, None] == domain_b[:, None, :]).astype(jnp.bfloat16)
        matched = jnp.einsum(
            "gjPl,gkl->gjPk", right_block, intersection, preferred_element_type=jnp.float32
        ).astype(jnp.bfloat16)
        exchange = jnp.einsum(
            "giPk,gjPk->gij", left_block, matched, preferred_element_type=jnp.float32
        ).astype(jnp.bfloat16)
        to_left = jnp.einsum(
            "gij,gjn->gin", exchange, right_vec, preferred_element_type=jnp.float32
        )
        to_right = jnp.einsum(
            "gij,gin->gjn", exchange, left_vec, preferred_element_type=jnp.float32
        )
        partial_value = partial_value.at[index_a].add(to_left)
        return partial_value.at[index_b].add(to_right * keep[:, None, None])

    partial_value = jnp.zeros((near_count, BS, vector_width), jnp.float32)
    partial_value = lax.fori_loop(0, pair_rows // pair_group, group_step, partial_value)
    by_offset = {}
    for offset in range(-REACH, REACH + 1):
        lower = (offset + REACH) * blocks_here
        by_offset[offset] = partial_value[lower : lower + blocks_here]
    result = by_offset[0]
    for offset in range(-REACH, REACH + 1):
        if offset != 0:
            result = result + shifted(by_offset[offset], "pair", offset)
    return lax.psum(result, "aux")


def solution(mesh):
    return jax.shard_map(
        local,
        mesh=mesh,
        in_specs=(P("pair", None, "aux", None), P("pair", None, None), P("pair", None), P(), P()),
        out_specs=P("pair", None, None),
        check_vma=False,
    )
```

profile of v0, /device:TPU:1, one launch (start us, length us, event | category | flops | bytes accessed | tf_op | source)
XLA Modules:
  0.0 429.0 jit_solution(12135149753040293294)
XLA Ops:
  6.6 1.6 reshape.38
  8.2 1.0 constant_dynamic-update-slice_fusion.1
  9.9 6.6 %collective-permute-start = (bf16[2,128,2176]{2,1,0:T(8,128)(2,1)}, bf16[2,128,2176]{2,1,0:T(8,128)(2,1)}, u32[]{:S(2)}, u32[]{:S(2)}) collective-permute-start(bf16[2,128,2176]{2,1,0:T(8,128)(2,1)} %constant_dynamic-update-slice_fusion), channel_id=1, source_target_pairs={{0,4},{2,6},{4,8},{6,10},{8,12},{10,14},{12,16},{14,18},{16,20},{1... | collective-permute-start | bytes 3342344 | tf_op jit(solution)/shard_map/ppermute | solution.py:16
  16.5 3.3 collective-permute-start.1
  19.8 1.3 collective-permute-start.2
  21.1 1.3 collective-permute-start.3
  23.7 15.4 %collective-permute-done = bf16[2,128,2176]{2,1,0:T(8,128)(2,1)} collective-permute-done((bf16[2,128,2176]{2,1,0:T(8,128)(2,1)}, bf16[2,128,2176]{2,1,0:T(8,128)(2,1)}, u32[]{:S(2)}, u32[]{:S(2)}) %collective-permute-start) | collective-permute-done | bytes 1114144 | tf_op jit(solution)/shard_map/ppermute | solution.py:16
  39.1 1.3 constant_dynamic-update-slice_fusion.7
  40.4 22.5 %collective-permute-done.1 = bf16[2,128,2176]{2,1,0:T(8,128)(2,1)} collective-permute-done((bf16[2,128,2176]{2,1,0:T(8,128)(2,1)}, bf16[2,128,2176]{2,1,0:T(8,128)(2,1)}, u32[]{:S(2)}, u32[]{:S(2)}) %collective-permute-start.1) | collective-permute-done | bytes 1114144 | tf_op jit(solution)/shard_map/ppermute | solution.py:16
  63.0 1.4 constant_dynamic-update-slice_fusion.6
  64.5 47.3 %collective-permute-done.2 = bf16[2,128,2176]{2,1,0:T(8,128)(2,1)} collective-permute-done((bf16[2,128,2176]{2,1,0:T(8,128)(2,1)}, bf16[2,128,2176]{2,1,0:T(8,128)(2,1)}, u32[]{:S(2)}, u32[]{:S(2)}) %collective-permute-start.2) | collective-permute-done | bytes 1114144 | tf_op jit(solution)/shard_map/ppermute | solution.py:16
  111.7 1.4 constant_dynamic-update-slice_fusion.3
  114.1 4.1 copy.24
  118.2 249.0 %while.13 = (s32[]{:T(128)}, f32[10,128,128]{2,1,0:T(8,128)S(1)}, s32[64,2]{0,1:T(2,128)S(1)}, bf16[10,128,16,128]{3,2,1,0:T(8,128)(2,1)}, s32[64,2,128]{2,0,1:T...) while((s32[]{:T(128)}, f32[10,128,128]{2,1,0:T(8,128)S(1)}, ...), condition=%wide.region_4.7_spmd, body=%wide.region_1.6_spmd.sunk | while | flops 1148061824 | bytes 48662328 | solution.py:78
  118.4 5.6 %gather_fusion.1 = bf16[8,128,16,128]{3,2,1,0:T(8,128)(2,1)} fusion(bf16[10,128,16,128]{3,2,1,0:T(8,128)(2,1)} %get-tuple-element.256, s32[1024]{0:T(1024)S(1)} %pad_clamp_fusion.6), kind=kCustom, calls=%fused_computation.clone.clone.1 | custom fusion | bytes 8388640 | tf_op jit(solution)/shard_map/while/body/eval_jaxpr/jit(_take)/gather | solution.py:57
  124.0 4.7 %broadcast_select_fusion.5 = bf16[8,128,16,128]{3,2,1,0:T(8,128)(2,1)} fusion(bf16[8,128,16,128]{3,2,1,0:T(8,128)(2,1)} %gather_fusion.1, pred[8]{0:T(512)(128)(4,1)S(1)} %get-tuple-element.225), kind=kLoop, calls=%fused_computation.13.clone.1 | loop fusion | flops 2097152 | bytes 8388616 | tf_op jit(solution)/shard_map/while/body/eval_jaxpr/jit(_take)/select_n | solution.py:57
  128.7 5.6 %gather_fusion = bf16[8,128,16,128]{3,2,1,0:T(8,128)(2,1)} fusion(bf16[10,128,16,128]{3,2,1,0:T(8,128)(2,1)} %get-tuple-element.256, s32[1024]{0:T(1024)S(1)} %pad_clamp_fusion.5), kind=kCustom, calls=%fused_computation.2.clone.clone.1 | custom fusion | bytes 8388640 | tf_op jit(solution)/shard_map/while/body/eval_jaxpr/jit(_take)/gather | solution.py:58
  134.3 4.7 %broadcast_select_fusion.4 = bf16[8,128,16,128]{3,2,1,0:T(8,128)(2,1)} fusion(bf16[8,128,16,128]{3,2,1,0:T(8,128)(2,1)} %gather_fusion, pred[8]{0:T(512)(128)(4,1)S(1)} %get-tuple-element.223), kind=kLoop, calls=%fused_computation.12.clone.1 | loop fusion | flops 2097152 | bytes 8388616 | tf_op jit(solution)/shard_map/while/body/eval_jaxpr/jit(_take)/select_n | solution.py:58
  139.0 6.3 %fusion.73 = bf16[8,128,128]{2,1,0:T(8,128)(2,1)S(1)} fusion(bf16[8,128,16,128]{3,2,1,0:T(8,128)(2,1)} %broadcast_select_fusion.4, bf16[8,128,16,128]{3,2,1,0:T(8,128)(2,1)} %broadcast_select_fusion.5, s32[8,128]{1,0:T(8,128)S(1)} %get-tuple-element.228, s32[8,128]{1,0:T(8,128)S(1)} %get-tuple-element.229), kind=kOutput, calls=%fused_computation.16.clone.1 | convolution fusion | flops 1076101120 | bytes 8658944 | tf_op jit(solution)/shard_map/while/body/eval_jaxpr/giPk,gjPk->gij/dot_general | solution.py:65
  149.5 5.6 %gather_fusion.1 = bf16[8,128,16,128]{3,2,1,0:T(8,128)(2,1)} fusion(bf16[10,128,16,128]{3,2,1,0:T(8,128)(2,1)} %get-tuple-element.256, s32[1024]{0:T(1024)S(1)} %pad_clamp_fusion.6), kind=kCustom, calls=%fused_computation.clone.clone.1 | custom fusion | bytes 8388640 | tf_op jit(solution)/shard_map/while/body/eval_jaxpr/jit(_take)/gather | solution.py:57
  155.1 4.7 %broadcast_select_fusion.5 = bf16[8,128,16,128]{3,2,1,0:T(8,128)(2,1)} fusion(bf16[8,128,16,128]{3,2,1,0:T(8,128)(2,1)} %gather_fusion.1, pred[8]{0:T(512)(128)(4,1)S(1)} %get-tuple-element.225), kind=kLoop, calls=%fused_computation.13.clone.1 | loop fusion | flops 2097152 | bytes 8388616 | tf_op jit(solution)/shard_map/while/body/eval_jaxpr/jit(_take)/select_n | solution.py:57
  159.8 5.6 %gather_fusion = bf16[8,128,16,128]{3,2,1,0:T(8,128)(2,1)} fusion(bf16[10,128,16,128]{3,2,1,0:T(8,128)(2,1)} %get-tuple-element.256, s32[1024]{0:T(1024)S(1)} %pad_clamp_fusion.5), kind=kCustom, calls=%fused_computation.2.clone.clone.1 | custom fusion | bytes 8388640 | tf_op jit(solution)/shard_map/while/body/eval_jaxpr/jit(_take)/gather | solution.py:58
  165.4 4.7 %broadcast_select_fusion.4 = bf16[8,128,16,128]{3,2,1,0:T(8,128)(2,1)} fusion(bf16[8,128,16,128]{3,2,1,0:T(8,128)(2,1)} %gather_fusion, pred[8]{0:T(512)(128)(4,1)S(1)} %get-tuple-element.223), kind=kLoop, calls=%fused_computation.12.clone.1 | loop fusion | flops 2097152 | bytes 8388616 | tf_op jit(solution)/shard_map/while/body/eval_jaxpr/jit(_take)/select_n | solution.py:58
  170.1 6.3 %fusion.73 = bf16[8,128,128]{2,1,0:T(8,128)(2,1)S(1)} fusion(bf16[8,128,16,128]{3,2,1,0:T(8,128)(2,1)} %broadcast_select_fusion.4, bf16[8,128,16,128]{3,2,1,0:T(8,128)(2,1)} %broadcast_select_fusion.5, s32[8,128]{1,0:T(8,128)S(1)} %get-tuple-element.228, s32[8,128]{1,0:T(8,128)S(1)} %get-tuple-element.229), kind=kOutput, calls=%fused_computation.16.clone.1 | convolution fusion | flops 1076101120 | bytes 8658944 | tf_op jit(solution)/shard_map/while/body/eval_jaxpr/giPk,gjPk->gij/dot_general | solution.py:65
  177.4 1.0 scatter_fusion
  180.6 5.6 %gather_fusion.1 = bf16[8,128,16,128]{3,2,1,0:T(8,128)(2,1)} fusion(bf16[10,128,16,128]{3,2,1,0:T(8,128)(2,1)} %get-tuple-element.256, s32[1024]{0:T(1024)S(1)} %pad_clamp_fusion.6), kind=kCustom, calls=%fused_computation.clone.clone.1 | custom fusion | bytes 8388640 | tf_op jit(solution)/shard_map/while/body/eval_jaxpr/jit(_take)/gather | solution.py:57
  186.2 4.7 %broadcast_select_fusion.5 = bf16[8,128,16,128]{3,2,1,0:T(8,128)(2,1)} fusion(bf16[8,128,16,128]{3,2,1,0:T(8,128)(2,1)} %gather_fusion.1, pred[8]{0:T(512)(128)(4,1)S(1)} %get-tuple-element.225), kind=kLoop, calls=%fused_computation.13.clone.1 | loop fusion | flops 2097152 | bytes 8388616 | tf_op jit(solution)/shard_map/while/body/eval_jaxpr/jit(_take)/select_n | solution.py:57
  191.0 5.6 %gather_fusion = bf16[8,128,16,128]{3,2,1,0:T(8,128)(2,1)} fusion(bf16[10,128,16,128]{3,2,1,0:T(8,128)(2,1)} %get-tuple-element.256, s32[1024]{0:T(1024)S(1)} %pad_clamp_fusion.5), kind=kCustom, calls=%fused_computation.2.clone.clone.1 | custom fusion | bytes 8388640 | tf_op jit(solution)/shard_map/while/body/eval_jaxpr/jit(_take)/gather | solution.py:58
  196.6 4.7 %broadcast_select_fusion.4 = bf16[8,128,16,128]{3,2,1,0:T(8,128)(2,1)} fusion(bf16[8,128,16,128]{3,2,1,0:T(8,128)(2,1)} %gather_fusion, pred[8]{0:T(512)(128)(4,1)S(1)} %get-tuple-element.223), kind=kLoop, calls=%fused_computation.12.clone.1 | loop fusion | flops 2097152 | bytes 8388616 | tf_op jit(solution)/shard_map/while/body/eval_jaxpr/jit(_take)/select_n | solution.py:58
  201.3 6.3 %fusion.73 = bf16[8,128,128]{2,1,0:T(8,128)(2,1)S(1)} fusion(bf16[8,128,16,128]{3,2,1,0:T(8,128)(2,1)} %broadcast_select_fusion.4, bf16[8,128,16,128]{3,2,1,0:T(8,128)(2,1)} %broadcast_select_fusion.5, s32[8,128]{1,0:T(8,128)S(1)} %get-tuple-element.228, s32[8,128]{1,0:T(8,128)S(1)} %get-tuple-element.229), kind=kOutput, calls=%fused_computation.16.clone.1 | convolution fusion | flops 1076101120 | bytes 8658944 | tf_op jit(solution)/shard_map/while/body/eval_jaxpr/giPk,gjPk->gij/dot_general | solution.py:65
  211.7 5.6 %gather_fusion.1 = bf16[8,128,16,128]{3,2,1,0:T(8,128)(2,1)} fusion(bf16[10,128,16,128]{3,2,1,0:T(8,128)(2,1)} %get-tuple-element.256, s32[1024]{0:T(1024)S(1)} %pad_clamp_fusion.6), kind=kCustom, calls=%fused_computation.clone.clone.1 | custom fusion | bytes 8388640 | tf_op jit(solution)/shard_map/while/body/eval_jaxpr/jit(_take)/gather | solution.py:57
  217.4 4.7 %broadcast_select_fusion.5 = bf16[8,128,16,128]{3,2,1,0:T(8,128)(2,1)} fusion(bf16[8,128,16,128]{3,2,1,0:T(8,128)(2,1)} %gather_fusion.1, pred[8]{0:T(512)(128)(4,1)S(1)} %get-tuple-element.225), kind=kLoop, calls=%fused_computation.13.clone.1 | loop fusion | flops 2097152 | bytes 8388616 | tf_op jit(solution)/shard_map/while/body/eval_jaxpr/jit(_take)/select_n | solution.py:57
  222.1 5.6 %gather_fusion = bf16[8,128,16,128]{3,2,1,0:T(8,128)(2,1)} fusion(bf16[10,128,16,128]{3,2,1,0:T(8,128)(2,1)} %get-tuple-element.256, s32[1024]{0:T(1024)S(1)} %pad_clamp_fusion.5), kind=kCustom, calls=%fused_computation.2.clone.clone.1 | custom fusion | bytes 8388640 | tf_op jit(solution)/shard_map/while/body/eval_jaxpr/jit(_take)/gather | solution.py:58
  227.7 4.7 %broadcast_select_fusion.4 = bf16[8,128,16,128]{3,2,1,0:T(8,128)(2,1)} fusion(bf16[8,128,16,128]{3,2,1,0:T(8,128)(2,1)} %gather_fusion, pred[8]{0:T(512)(128)(4,1)S(1)} %get-tuple-element.223), kind=kLoop, calls=%fused_computation.12.clone.1 | loop fusion | flops 2097152 | bytes 8388616 | tf_op jit(solution)/shard_map/while/body/eval_jaxpr/jit(_take)/select_n | solution.py:58
  232.4 6.3 %fusion.73 = bf16[8,128,128]{2,1,0:T(8,128)(2,1)S(1)} fusion(bf16[8,128,16,128]{3,2,1,0:T(8,128)(2,1)} %broadcast_select_fusion.4, bf16[8,128,16,128]{3,2,1,0:T(8,128)(2,1)} %broadcast_select_fusion.5, s32[8,128]{1,0:T(8,128)S(1)} %get-tuple-element.228, s32[8,128]{1,0:T(8,128)S(1)} %get-tuple-element.229), kind=kOutput, calls=%fused_computation.16.clone.1 | convolution fusion | flops 1076101120 | bytes 8658944 | tf_op jit(solution)/shard_map/while/body/eval_jaxpr/giPk,gjPk->gij/dot_general | solution.py:65
  241.7 1.0 scatter_fusion.1
  242.9 5.6 %gather_fusion.1 = bf16[8,128,16,128]{3,2,1,0:T(8,128)(2,1)} fusion(bf16[10,128,16,128]{3,2,1,0:T(8,128)(2,1)} %get-tuple-element.256, s32[1024]{0:T(1024)S(1)} %pad_clamp_fusion.6), kind=kCustom, calls=%fused_computation.clone.clone.1 | custom fusion | bytes 8388640 | tf_op jit(solution)/shard_map/while/body/eval_jaxpr/jit(_take)/gather | solution.py:57
  248.5 4.7 %broadcast_select_fusion.5 = bf16[8,128,16,128]{3,2,1,0:T(8,128)(2,1)} fusion(bf16[8,128,16,128]{3,2,1,0:T(8,128)(2,1)} %gather_fusion.1, pred[8]{0:T(512)(128)(4,1)S(1)} %get-tuple-element.225), kind=kLoop, calls=%fused_computation.13.clone.1 | loop fusion | flops 2097152 | bytes 8388616 | tf_op jit(solution)/shard_map/while/body/eval_jaxpr/jit(_take)/select_n | solution.py:57
  253.2 5.6 %gather_fusion = bf16[8,128,16,128]{3,2,1,0:T(8,128)(2,1)} fusion(bf16[10,128,16,128]{3,2,1,0:T(8,128)(2,1)} %get-tuple-element.256, s32[1024]{0:T(1024)S(1)} %pad_clamp_fusion.5), kind=kCustom, calls=%fused_computation.2.clone.clone.1 | custom fusion | bytes 8388640 | tf_op jit(solution)/shard_map/while/body/eval_jaxpr/jit(_take)/gather | solution.py:58
  258.8 4.7 %broadcast_select_fusion.4 = bf16[8,128,16,128]{3,2,1,0:T(8,128)(2,1)} fusion(bf16[8,128,16,128]{3,2,1,0:T(8,128)(2,1)} %gather_fusion, pred[8]{0:T(512)(128)(4,1)S(1)} %get-tuple-element.223), kind=kLoop, calls=%fused_computation.12.clone.1 | loop fusion | flops 2097152 | bytes 8388616 | tf_op jit(solution)/shard_map/while/body/eval_jaxpr/jit(_take)/select_n | solution.py:58
  263.5 6.2 %fusion.73 = bf16[8,128,128]{2,1,0:T(8,128)(2,1)S(1)} fusion(bf16[8,128,16,128]{3,2,1,0:T(8,128)(2,1)} %broadcast_select_fusion.4, bf16[8,128,16,128]{3,2,1,0:T(8,128)(2,1)} %broadcast_select_fusion.5, s32[8,128]{1,0:T(8,128)S(1)} %get-tuple-element.228, s32[8,128]{1,0:T(8,128)S(1)} %get-tuple-element.229), kind=kOutput, calls=%fused_computation.16.clone.1 | convolution fusion | flops 1076101120 | bytes 8658944 | tf_op jit(solution)/shard_map/while/body/eval_jaxpr/giPk,gjPk->gij/dot_general | solution.py:65
  270.8 1.0 scatter_fusion
  274.0 5.6 %gather_fusion.1 = bf16[8,128,16,128]{3,2,1,0:T(8,128)(2,1)} fusion(bf16[10,128,16,128]{3,2,1,0:T(8,128)(2,1)} %get-tuple-element.256, s32[1024]{0:T(1024)S(1)} %pad_clamp_fusion.6), kind=kCustom, calls=%fused_computation.clone.clone.1 | custom fusion | bytes 8388640 | tf_op jit(solution)/shard_map/while/body/eval_jaxpr/jit(_take)/gather | solution.py:57
  279.6 4.7 %broadcast_select_fusion.5 = bf16[8,128,16,128]{3,2,1,0:T(8,128)(2,1)} fusion(bf16[8,128,16,128]{3,2,1,0:T(8,128)(2,1)} %gather_fusion.1, pred[8]{0:T(512)(128)(4,1)S(1)} %get-tuple-element.225), kind=kLoop, calls=%fused_computation.13.clone.1 | loop fusion | flops 2097152 | bytes 8388616 | tf_op jit(solution)/shard_map/while/body/eval_jaxpr/jit(_take)/select_n | solution.py:57
  284.3 5.6 %gather_fusion = bf16[8,128,16,128]{3,2,1,0:T(8,128)(2,1)} fusion(bf16[10,128,16,128]{3,2,1,0:T(8,128)(2,1)} %get-tuple-element.256, s32[1024]{0:T(1024)S(1)} %pad_clamp_fusion.5), kind=kCustom, calls=%fused_computation.2.clone.clone.1 | custom fusion | bytes 8388640 | tf_op jit(solution)/shard_map/while/body/eval_jaxpr/jit(_take)/gather | solution.py:58
  289.9 4.7 %broadcast_select_fusion.4 = bf16[8,128,16,128]{3,2,1,0:T(8,128)(2,1)} fusion(bf16[8,128,16,128]{3,2,1,0:T(8,128)(2,1)} %gather_fusion, pred[8]{0:T(512)(128)(4,1)S(1)} %get-tuple-element.223), kind=kLoop, calls=%fused_computation.12.clone.1 | loop fusion | flops 2097152 | bytes 8388616 | tf_op jit(solution)/shard_map/while/body/eval_jaxpr/jit(_take)/select_n | solution.py:58
  294.6 6.3 %fusion.73 = bf16[8,128,128]{2,1,0:T(8,128)(2,1)S(1)} fusion(bf16[8,128,16,128]{3,2,1,0:T(8,128)(2,1)} %broadcast_select_fusion.4, bf16[8,128,16,128]{3,2,1,0:T(8,128)(2,1)} %broadcast_select_fusion.5, s32[8,128]{1,0:T(8,128)S(1)} %get-tuple-element.228, s32[8,128]{1,0:T(8,128)S(1)} %get-tuple-element.229), kind=kOutput, calls=%fused_computation.16.clone.1 | convolution fusion | flops 1076101120 | bytes 8658944 | tf_op jit(solution)/shard_map/while/body/eval_jaxpr/giPk,gjPk->gij/dot_general | solution.py:65
  305.1 5.6 %gather_fusion.1 = bf16[8,128,16,128]{3,2,1,0:T(8,128)(2,1)} fusion(bf16[10,128,16,128]{3,2,1,0:T(8,128)(2,1)} %get-tuple-element.256, s32[1024]{0:T(1024)S(1)} %pad_clamp_fusion.6), kind=kCustom, calls=%fused_computation.clone.clone.1 | custom fusion | bytes 8388640 | tf_op jit(solution)/shard_map/while/body/eval_jaxpr/jit(_take)/gather | solution.py:57
  310.7 4.7 %broadcast_select_fusion.5 = bf16[8,128,16,128]{3,2,1,0:T(8,128)(2,1)} fusion(bf16[8,128,16,128]{3,2,1,0:T(8,128)(2,1)} %gather_fusion.1, pred[8]{0:T(512)(128)(4,1)S(1)} %get-tuple-element.225), kind=kLoop, calls=%fused_computation.13.clone.1 | loop fusion | flops 2097152 | bytes 8388616 | tf_op jit(solution)/shard_map/while/body/eval_jaxpr/jit(_take)/select_n | solution.py:57
  315.5 5.6 %gather_fusion = bf16[8,128,16,128]{3,2,1,0:T(8,128)(2,1)} fusion(bf16[10,128,16,128]{3,2,1,0:T(8,128)(2,1)} %get-tuple-element.256, s32[1024]{0:T(1024)S(1)} %pad_clamp_fusion.5), kind=kCustom, calls=%fused_computation.2.clone.clone.1 | custom fusion | bytes 8388640 | tf_op jit(solution)/shard_map/while/body/eval_jaxpr/jit(_take)/gather | solution.py:58
  321.1 4.7 %broadcast_select_fusion.4 = bf16[8,128,16,128]{3,2,1,0:T(8,128)(2,1)} fusion(bf16[8,128,16,128]{3,2,1,0:T(8,128)(2,1)} %gather_fusion, pred[8]{0:T(512)(128)(4,1)S(1)} %get-tuple-element.223), kind=kLoop, calls=%fused_computation.12.clone.1 | loop fusion | flops 2097152 | bytes 8388616 | tf_op jit(solution)/shard_map/while/body/eval_jaxpr/jit(_take)/select_n | solution.py:58
  325.8 6.3 %fusion.73 = bf16[8,128,128]{2,1,0:T(8,128)(2,1)S(1)} fusion(bf16[8,128,16,128]{3,2,1,0:T(8,128)(2,1)} %broadcast_select_fusion.4, bf16[8,128,16,128]{3,2,1,0:T(8,128)(2,1)} %broadcast_select_fusion.5, s32[8,128]{1,0:T(8,128)S(1)} %get-tuple-element.228, s32[8,128]{1,0:T(8,128)S(1)} %get-tuple-element.229), kind=kOutput, calls=%fused_computation.16.clone.1 | convolution fusion | flops 1076101120 | bytes 8658944 | tf_op jit(solution)/shard_map/while/body/eval_jaxpr/giPk,gjPk->gij/dot_general | solution.py:65
  336.2 5.6 %gather_fusion.1 = bf16[8,128,16,128]{3,2,1,0:T(8,128)(2,1)} fusion(bf16[10,128,16,128]{3,2,1,0:T(8,128)(2,1)} %get-tuple-element.256, s32[1024]{0:T(1024)S(1)} %pad_clamp_fusion.6), kind=kCustom, calls=%fused_computation.clone.clone.1 | custom fusion | bytes 8388640 | tf_op jit(solution)/shard_map/while/body/eval_jaxpr/jit(_take)/gather | solution.py:57
  341.9 4.7 %broadcast_select_fusion.5 = bf16[8,128,16,128]{3,2,1,0:T(8,128)(2,1)} fusion(bf16[8,128,16,128]{3,2,1,0:T(8,128)(2,1)} %gather_fusion.1, pred[8]{0:T(512)(128)(4,1)S(1)} %get-tuple-element.225), kind=kLoop, calls=%fused_computation.13.clone.1 | loop fusion | flops 2097152 | bytes 8388616 | tf_op jit(solution)/shard_map/while/body/eval_jaxpr/jit(_take)/select_n | solution.py:57
  346.6 5.6 %gather_fusion = bf16[8,128,16,128]{3,2,1,0:T(8,128)(2,1)} fusion(bf16[10,128,16,128]{3,2,1,0:T(8,128)(2,1)} %get-tuple-element.256, s32[1024]{0:T(1024)S(1)} %pad_clamp_fusion.5), kind=kCustom, calls=%fused_computation.2.clone.clone.1 | custom fusion | bytes 8388640 | tf_op jit(solution)/shard_map/while/body/eval_jaxpr/jit(_take)/gather | solution.py:58
  352.2 4.7 %broadcast_select_fusion.4 = bf16[8,128,16,128]{3,2,1,0:T(8,128)(2,1)} fusion(bf16[8,128,16,128]{3,2,1,0:T(8,128)(2,1)} %gather_fusion, pred[8]{0:T(512)(128)(4,1)S(1)} %get-tuple-element.223), kind=kLoop, calls=%fused_computation.12.clone.1 | loop fusion | flops 2097152 | bytes 8388616 | tf_op jit(solution)/shard_map/while/body/eval_jaxpr/jit(_take)/select_n | solution.py:58
  356.9 6.3 %fusion.73 = bf16[8,128,128]{2,1,0:T(8,128)(2,1)S(1)} fusion(bf16[8,128,16,128]{3,2,1,0:T(8,128)(2,1)} %broadcast_select_fusion.4, bf16[8,128,16,128]{3,2,1,0:T(8,128)(2,1)} %broadcast_select_fusion.5, s32[8,128]{1,0:T(8,128)S(1)} %get-tuple-element.228, s32[8,128]{1,0:T(8,128)S(1)} %get-tuple-element.229), kind=kOutput, calls=%fused_computation.16.clone.1 | convolution fusion | flops 1076101120 | bytes 8658944 | tf_op jit(solution)/shard_map/while/body/eval_jaxpr/giPk,gjPk->gij/dot_general | solution.py:65
  367.3 1.3 collective-permute-start.4
  368.6 1.3 collective-permute-start.5
  369.9 4.0 collective-permute-start.6
  373.9 5.5 %collective-permute-start.7 = (f32[2,128,128]{2,1,0:T(8,128)S(1)}, f32[2,128,128]{2,1,0:T(8,128)S(1)}, u32[]{:S(2)}, u32[]{:S(2)}) collective-permute-start(f32[2,128,128]{2,1,0:T(8,128)S(1)} %get-tuple-element.161), channel_id=1, source_target_pairs={{0,4},{2,6},{4,8},{6,10},{8,12},{10,14},{12,16},{14,18},{16,20},{1... | collective-permute-start | bytes 393224 | tf_op jit(solution)/shard_map/ppermute | solution.py:16
  379.4 1.9 collective-permute-done.7
  382.0 38.5 %all-reduce.2.cloned.1.call-done = f32[2,128,128]{2,1,0:T(8,128)} async-done(((f32[2,128,128]{2,1,0:T(8,128)}), f32[2,128,128]{2,1,0:T(8,128)}) %all-reduce.2.cloned.1.call-update) | async-done | bytes 131088 | tf_op jit(solution)/shard_map/psum | solution.py:87
  420.5 1.6 copy.61
  (142 shorter events, 33.7 us)
Async XLA Ops:
  6.5 16.2 %copy-start = (s32[256,128]{1,0:T(8,128)S(1)}, s32[256,128]{1,0:T(8,128)}, u32[]{:S(2)}) copy-start(s32[256,128]{1,0:T(8,128)} %param.15) | copy-start | bytes 393220
  6.5 2.7 copy-start.1
  6.5 15.9 %copy-start.2 = (s32[64,2]{0,1:T(2,128)S(1)}, s32[64,2]{0,1:T(2,128)}, u32[]{:S(2)}) copy-start(s32[64,2]{0,1:T(2,128)} %param.13) | copy-start | bytes 1540
  6.5 16.8 %copy-start.3 = (s32[256]{0:T(256)S(1)}, s32[256]{0:T(256)}, u32[]{:S(2)}) copy-start(s32[256]{0:T(256)} %param.14) | copy-start | bytes 3076
  6.5 414.0 %all-reduce.2.cloned.1.call-start = ((), (), s32[]{:S(2)}) async-start(), calls=%async_computation | async-start | bytes 262144 | tf_op jit(solution)/shard_map/psum | solution.py:87
  9.9 29.2 %collective-permute-start = (bf16[2,128,2176]{2,1,0:T(8,128)(2,1)}, bf16[2,128,2176]{2,1,0:T(8,128)(2,1)}, u32[]{:S(2)}, u32[]{:S(2)}) collective-permute-start(bf16[2,128,2176]{2,1,0:T(8,128)(2,1)} %constant_dynamic-update-slice_fusion), channel_id=1, source_target_pairs={{0,4},{2,6},{4,8},{6,10},{8,12},{10,14},{12,16},{14,18},{16,20},{1... | collective-permute-start | bytes 3342344 | tf_op jit(solution)/shard_map/ppermute | solution.py:16
  16.5 46.4 %collective-permute-start.1 = (bf16[2,128,2176]{2,1,0:T(8,128)(2,1)}, bf16[2,128,2176]{2,1,0:T(8,128)(2,1)}, u32[]{:S(2)}, u32[]{:S(2)}) collective-permute-start(bf16[2,128,2176]{2,1,0:T(8,128)(2,1)} %constant_dynamic-update-slice_fusion), channel_id=1, source_target_pairs={{0,2},{2,4},{4,6},{6,8},{8,10},{10,12},{12,14},{14,16},{16,18},{18... | collective-permute-start | bytes 3342344 | tf_op jit(solution)/shard_map/ppermute | solution.py:16
  19.8 91.9 %collective-permute-start.2 = (bf16[2,128,2176]{2,1,0:T(8,128)(2,1)}, bf16[2,128,2176]{2,1,0:T(8,128)(2,1)}, u32[]{:S(2)}, u32[]{:S(2)}) collective-permute-start(bf16[2,128,2176]{2,1,0:T(8,128)(2,1)} %constant_dynamic-update-slice_fusion), channel_id=1, source_target_pairs={{2,0},{4,2},{6,4},{8,6},{10,8},{12,10},{14,12},{16,14},{18,16},{20... | collective-permute-start | bytes 3342344 | tf_op jit(solution)/shard_map/ppermute | solution.py:16
  21.1 92.0 %collective-permute-start.3 = (bf16[2,128,2176]{2,1,0:T(8,128)(2,1)}, bf16[2,128,2176]{2,1,0:T(8,128)(2,1)S(1)}, u32[]{:S(2)}, u32[]{:S(2)}) collective-permute-start(bf16[2,128,2176]{2,1,0:T(8,128)(2,1)} %constant_dynamic-update-slice_fusion), channel_id=1, source_target_pairs={{4,0},{6,2},{8,4},{10,6},{12,8},{14,10},{16,12},{18,14},{20,16},{2... | collective-permute-start | bytes 3342344 | tf_op jit(solution)/shard_map/ppermute | solution.py:16
  367.3 12.1 %collective-permute-start.4 = (f32[2,128,128]{2,1,0:T(8,128)S(1)}, f32[2,128,128]{2,1,0:T(8,128)S(1)}, u32[]{:S(2)}, u32[]{:S(2)}) collective-permute-start(f32[2,128,128]{2,1,0:T(8,128)S(1)} %get-tuple-element.160), channel_id=1, source_target_pairs={{4,0},{6,2},{8,4},{10,6},{12,8},{14,10},{16,12},{18,14},{20,16},{2... | collective-permute-start | bytes 393224 | tf_op jit(solution)/shard_map/ppermute | solution.py:16
  368.6 10.8 %collective-permute-start.5 = (f32[2,128,128]{2,1,0:T(8,128)S(1)}, f32[2,128,128]{2,1,0:T(8,128)S(1)}, u32[]{:S(2)}, u32[]{:S(2)}) collective-permute-start(f32[2,128,128]{2,1,0:T(8,128)S(1)} %get-tuple-element.163), channel_id=1, source_target_pairs={{2,0},{4,2},{6,4},{8,6},{10,8},{12,10},{14,12},{16,14},{18,16},{20... | collective-permute-start | bytes 393224 | tf_op jit(solution)/shard_map/ppermute | solution.py:16
  369.9 9.5 %collective-permute-start.6 = (f32[2,128,128]{2,1,0:T(8,128)S(1)}, f32[2,128,128]{2,1,0:T(8,128)S(1)}, u32[]{:S(2)}, u32[]{:S(2)}) collective-permute-start(f32[2,128,128]{2,1,0:T(8,128)S(1)} %get-tuple-element.162), channel_id=1, source_target_pairs={{0,2},{2,4},{4,6},{6,8},{8,10},{10,12},{12,14},{14,16},{16,18},{18... | collective-permute-start | bytes 393224 | tf_op jit(solution)/shard_map/ppermute | solution.py:16
  373.9 7.4 %collective-permute-start.7 = (f32[2,128,128]{2,1,0:T(8,128)S(1)}, f32[2,128,128]{2,1,0:T(8,128)S(1)}, u32[]{:S(2)}, u32[]{:S(2)}) collective-permute-start(f32[2,128,128]{2,1,0:T(8,128)S(1)} %get-tuple-element.161), channel_id=1, source_target_pairs={{0,4},{2,6},{4,8},{6,10},{8,12},{10,14},{12,16},{14,18},{16,20},{1... | collective-permute-start | bytes 393224 | tf_op jit(solution)/shard_map/ppermute | solution.py:16
Sparse Core Ops, SparseCore 0:
  382.1 38.3 all-reduce.1
where the time goes:
time: 431 us; the launch traced here: 429 us
  waiting for transfers between devices  126 us (29%)
  local copies, waits for them, and re-layouts  115 us (27%)
  other arithmetic  94.1 us (22%)
  matrix products  55 us (13%)
  starting transfers between devices  24.6 us (6%)
  between operations  13.6 us (3%)
    ppermute x8, waiting for transfers between devices, shifted(): return lax.ppermute(shard, axis, pairs)  87.1 us
    dot_general x8, matrix products, group_step(): jnp.einsum('giPk,gjPk->gij', left_block, matched, preferred_element_type=...  50.1 us
    gather x8, local copies, waits for them, and re-layouts, group_step(): left_block = jnp.take(near_blocks, index_a, axis=0)  45.1 us
    gather x8, local copies, waits for them, and re-layouts, group_step(): right_block = jnp.take(near_blocks, index_b, axis=0)  44.8 us
    psum x1, waiting for transfers between devices, local(): return lax.psum(result, 'aux')  38.5 us
    select_n x8, other arithmetic, group_step(): left_block = jnp.take(near_blocks, index_a, axis=0)  37.8 us
    select_n x8, other arithmetic, group_step(): right_block = jnp.take(near_blocks, index_b, axis=0)  37.4 us
    ppermute x8, starting transfers between devices, shifted(): return lax.ppermute(shard, axis, pairs)  24.6 us
  transfers between devices with their start and end apart: 9, of which 5 were waited for; matrix products, arithmetic and copies ran while one was open for 1% of the time, Pallas kernels for 0%

commit v1 on v0

v1 whole, which is shorter than its diff:
```python
import jax
import jax.numpy as jnp
from jax import lax
from jax.experimental import pallas as pl
from jax.experimental.pallas import tpu as pltpu
from jax.sharding import PartitionSpec as P

MESH = pl.DeviceIdType.MESH
BS = 128
BLK = 2
PLANE = 16
PLANES = 8
AUXW = 16
HALO = 4
SPAN = 2 * HALO + 1
WIN = PLANE + 2 * HALO
SLOTS = WIN * BLK
MSG = BLK * BS
DEPTH = SPAN * MSG


def dot(a, b, dims=((1,), (0,))):
    return lax.dot_general(a, b, (dims, ((), ())), preferred_element_type=jnp.float32)


def kernel(b_hbm, v_hbm, pt_ref, slot_ref, dom_ref, out_ref,
           braw, vloc, bf32, bt, ysend, yw, cntsend, cnt, nown, nz, nx, domax, dombx, mall,
           wsend, wr, acc, other,
           load_sem, own_sem, cs_sem, cr_sem, ns_sem, nr_sem, ys_sem, yr_sem, zs_sem, zr_sem,
           ws_sem, wr_sem, os_sem, or_sem):
    me = lax.axis_index("pair")
    core = lax.axis_index("aux")
    z = me // PLANE
    g = me % PLANE
    base = z * PLANE
    up = ((z + 1) % PLANES) * PLANE + g
    down = ((z + PLANES - 1) % PLANES) * PLANE + g
    slot_base = base * BLK - HALO * BLK

    def peer(d):
        return (g + d) % PLANE

    load_v = pltpu.make_async_copy(v_hbm, vloc, load_sem.at[0])
    load_b = pltpu.make_async_copy(b_hbm, braw, load_sem.at[1])
    load_v.start()
    load_b.start()

    barrier = pltpu.get_barrier_semaphore()

    def greet(d, carry):
        pl.semaphore_signal(barrier, inc=1, device_id=(base + peer(d), core), device_id_type=MESH)
        return carry

    lax.fori_loop(1, PLANE, greet, 0)
    pl.semaphore_signal(barrier, inc=1, device_id=(up, core), device_id_type=MESH)
    pl.semaphore_signal(barrier, inc=1, device_id=(down, core), device_id_type=MESH)
    pl.semaphore_signal(barrier, inc=1, device_id=(me, 1 - core), device_id_type=MESH)

    slot_row = slot_ref[...]
    pair_rows = pt_ref.shape[0]
    numbers = lax.broadcasted_iota(jnp.int32, (pair_rows, slot_row.shape[1]), 1)
    slot_f = slot_row.astype(jnp.float32)
    pt = pt_ref[...]

    def slot_of(column):
        return jnp.sum(jnp.where(pt[:, column:column + 1] == numbers, slot_f, 0.0), axis=1, keepdims=True)

    slot_a, slot_b = slot_of(0), slot_of(1)
    lane = lax.broadcasted_iota(jnp.int32, (pair_rows, 128), 1).astype(jnp.float32) + slot_base.astype(jnp.float32)
    one_a = (slot_a == lane).astype(jnp.float32)
    one_b = (slot_b == lane).astype(jnp.float32)
    keep = (slot_a != slot_b).astype(jnp.float32)
    counts = dot(one_a.astype(jnp.bfloat16), one_b.astype(jnp.bfloat16), ((0,), (0,)))
    counts = counts + dot((one_b * keep).astype(jnp.bfloat16), one_a.astype(jnp.bfloat16), ((0,), (0,)))
    counts = counts[:SLOTS].astype(jnp.bfloat16)
    cntsend[...] = counts
    cnt[g] = counts

    slot_iota = lax.broadcasted_iota(jnp.int32, (SLOTS, slot_row.shape[1]), 0) + slot_base
    pick = (slot_iota == slot_row).astype(jnp.float32).astype(jnp.bfloat16)
    dom = dom_ref[...]
    dom_high = (dom // 128).astype(jnp.float32).astype(jnp.bfloat16)
    dom_low = (dom % 128).astype(jnp.float32).astype(jnp.bfloat16)
    dom_win = dot(pick, dom_high) * 128.0 + dot(pick, dom_low)
    dom_t = jnp.concatenate([dom_win, jnp.zeros((128 - SLOTS, 128), jnp.float32)], axis=0).T
    for a in range(PLANE * BLK):
        column = dom_t[:, HALO * BLK + a:HALO * BLK + a + 1]
        domax[a] = jnp.broadcast_to(column, (128, 128)).astype(jnp.int32).astype(jnp.int16)
    for s in range(SLOTS):
        dombx[s] = jnp.broadcast_to(dom_win[s:s + 1], (16, 128)).astype(jnp.int32).astype(jnp.int16)

    load_v.wait()
    load_b.wait()
    for k in range(BLK):
        bf32[...] = braw[k].astype(jnp.float32)
        for p in range(AUXW):
            part = bf32[pl.ds(p, BS, stride=AUXW), :].astype(jnp.bfloat16)
            bt[k, p] = part
            ysend[p, k * BS:(k + 1) * BS, :] = dot(part, vloc[k], ((0,), (0,))).astype(jnp.bfloat16)
    own_y = pltpu.make_async_copy(ysend.at[g], yw.at[pl.ds((HALO + g) * MSG, MSG)], own_sem.at[0])
    own_y.start()

    pl.semaphore_wait(barrier, PLANE + 2)

    def count_copy(d, to):
        return pltpu.make_async_remote_copy(
            cntsend, cnt.at[g if to else peer(d)], cs_sem.at[peer(d)], cr_sem.at[g if to else peer(d)],
            device_id=(base + peer(d), core), device_id_type=MESH)

    def y_copy(d, to):
        row = g if to else peer(d)
        return pltpu.make_async_remote_copy(
            ysend.at[peer(d)], yw.at[pl.ds((HALO + row) * MSG, MSG)], ys_sem.at[peer(d)], yr_sem.at[row],
            device_id=(base + peer(d), core), device_id_type=MESH)

    def loop(lower, upper, body):
        def step(d, carry):
            body(d)
            return carry
        lax.fori_loop(lower, upper, step, 0)

    loop(1, PLANE, lambda d: count_copy(d, True).start())
    loop(1, PLANE, lambda d: y_copy(d, True).start())

    loop(1, PLANE, lambda d: count_copy(d, False).wait_recv())
    total = jnp.sum(cnt[...].astype(jnp.float32), axis=0)
    nown[...] = total
    n_up = pltpu.make_async_remote_copy(nown, nz.at[0], ns_sem.at[0], nr_sem.at[0],
                                        device_id=(up, core), device_id_type=MESH)
    n_down = pltpu.make_async_remote_copy(nown, nz.at[1], ns_sem.at[1], nr_sem.at[1],
                                          device_id=(down, core), device_id_type=MESH)
    n_up.start()
    n_down.start()

    def spread(matrix):
        for s in range(SLOTS):
            nx[s] = jnp.broadcast_to(matrix[HALO * BLK:HALO * BLK + PLANE * BLK, s:s + 1], (PLANE * BLK, 128))

    def build(i):
        for k in range(BLK):
            a = i * BLK + k
            left = domax[a]
            for s in range(SPAN * BLK):
                weight = jnp.broadcast_to(nx[i * BLK + s, pl.ds(a, 1), :], (16, 128)).astype(jnp.bfloat16)
                right = dombx[i * BLK + s]
                for h in range(BS // 16):
                    tile = jnp.where(left[h * 16:(h + 1) * 16] == right, weight, jnp.bfloat16(0))
                    mall[i, k * BS + h * 16:k * BS + (h + 1) * 16, s * BS:(s + 1) * BS] = tile

    spread(total)
    loop(HALO, PLANE - HALO, build)

    n_up.wait()
    n_down.wait()
    shift = PLANE * BLK
    wide = SLOTS - shift
    low, high = nz[0], nz[1]
    lanes = lax.broadcasted_iota(jnp.int32, (wide, 128), 1)
    from_low = jnp.where(lanes < wide, pltpu.roll(low[shift:], 128 - shift, 1), 0.0)
    from_high = jnp.where((lanes >= shift) & (lanes < SLOTS), pltpu.roll(high[:wide], shift, 1), 0.0)
    total = total + jnp.concatenate([from_low, jnp.zeros((SLOTS - 2 * wide, 128), jnp.float32), from_high], axis=0)
    spread(total)
    loop(0, HALO, build)
    loop(PLANE - HALO, PLANE, build)

    own_y.wait()

    def wait_y(s):
        @pl.when(s != g)
        def _():
            d = (s + PLANE - g) % PLANE
            y_copy(d, False).wait_recv()

    loop(PLANE - HALO, PLANE, wait_y)
    z_up = pltpu.make_async_remote_copy(
        yw.at[pl.ds(PLANE * MSG, HALO * MSG)], yw.at[pl.ds(0, HALO * MSG)], zs_sem.at[0], zr_sem.at[0],
        device_id=(up, core), device_id_type=MESH)
    z_up.start()
    loop(0, HALO, wait_y)
    z_down = pltpu.make_async_remote_copy(
        yw.at[pl.ds(HALO * MSG, HALO * MSG)], yw.at[pl.ds((HALO + PLANE) * MSG, HALO * MSG)],
        zs_sem.at[1], zr_sem.at[1], device_id=(down, core), device_id_type=MESH)
    z_down.start()
    loop(HALO, PLANE - HALO, wait_y)

    def w_copy(i, source):
        return pltpu.make_async_remote_copy(
            wsend.at[i], wr.at[source], ws_sem.at[i], wr_sem.at[source],
            device_id=(base + i, core), device_id_type=MESH)

    def apply_index(i):
        w = dot(mall[i], yw[pl.ds(i * MSG, DEPTH), :]).astype(jnp.bfloat16)
        wsend[i] = w

        @pl.when(i != g)
        def _():
            w_copy(i, g).start()

    half = PLANE // 2
    loop(0, half, lambda t: apply_index(HALO + (g + t) % half))
    z_up.wait()
    z_down.wait()

    def outer(t):
        j = (g + t) % half
        apply_index(j + half * (j // HALO))

    loop(0, half, outer)

    def add(source):
        def block(k, first):
            return dot(bt[k, source], first)
        for k in range(BLK):
            acc[k] += dot(bt[k, source], wr[source, k * BS:(k + 1) * BS, :])

    own_w = pltpu.make_async_copy(wsend.at[g], wr.at[g], own_sem.at[1])
    own_w.start()
    acc[...] = jnp.zeros_like(acc)
    own_w.wait()
    add(g)

    def collect(t):
        d = PLANE - t
        source = peer(d)
        w_copy(source, source).wait_recv()
        add(source)

    loop(1, PLANE, collect)

    swap = pltpu.make_async_remote_copy(acc, other, os_sem, or_sem,
                                        device_id=(me, 1 - core), device_id_type=MESH)
    swap.start()

    loop(1, PLANE, lambda d: count_copy(d, True).wait_send())
    loop(1, PLANE, lambda d: y_copy(d, True).wait_send())
    loop(1, PLANE, lambda d: w_copy(peer(d), g).wait_send())
    swap.wait()
    out_ref[...] = acc[...] + other[...]


def local(half_transformed, trials, pair_table, block_slot, domains):
    blocks = half_transformed.shape[0]
    vmem = pl.BlockSpec(memory_space=pltpu.VMEM)
    hbm = pl.BlockSpec(memory_space=pl.ANY)
    bf, f32 = jnp.bfloat16, jnp.float32
    dma = pltpu.SemaphoreType.DMA
    scratch = [
        pltpu.VMEM((BLK, BS * AUXW, 128), bf),
        pltpu.VMEM((BLK, BS, 128), bf),
        pltpu.VMEM((BS * AUXW, 128), f32),
        pltpu.VMEM((BLK, AUXW, BS, 128), bf),
        pltpu.VMEM((AUXW, MSG, 128), bf),
        pltpu.VMEM((WIN * MSG, 128), bf),
        pltpu.VMEM((SLOTS, 128), bf),
        pltpu.VMEM((PLANE, SLOTS, 128), bf),
        pltpu.VMEM((SLOTS, 128), f32),
        pltpu.VMEM((2, SLOTS, 128), f32),
        pltpu.VMEM((SLOTS, PLANE * BLK, 128), f32),
        pltpu.VMEM((PLANE * BLK, 128, 128), jnp.int16),
        pltpu.VMEM((SLOTS, 16, 128), jnp.int16),
        pltpu.VMEM((PLANE, MSG, DEPTH), bf),
        pltpu.VMEM((PLANE, MSG, 128), bf),
        pltpu.VMEM((AUXW, MSG, 128), bf),
        pltpu.VMEM((BLK, BS, 128), f32),
        pltpu.VMEM((BLK, BS, 128), f32),
        dma((2,)), dma((2,)), dma((PLANE,)), dma((PLANE,)), dma((2,)), dma((2,)),
        dma((PLANE,)), dma((PLANE,)), dma((2,)), dma((2,)), dma((PLANE,)), dma((PLANE,)), dma, dma,
    ]
    return pl.pallas_call(
        kernel,
        out_shape=jax.ShapeDtypeStruct(trials.shape, f32),
        in_specs=[hbm, hbm, vmem, vmem, vmem],
        out_specs=vmem,
        scratch_shapes=scratch,
        compiler_params=pltpu.CompilerParams(collective_id=1, has_side_effects=True, vmem_limit_bytes=50 << 20),
        name="exchange",
    )(half_transformed.reshape(blocks, BS * AUXW, 128), trials, pair_table,
      block_slot.reshape(1, -1), domains)


def solution(mesh):
    return jax.shard_map(
        local,
        mesh=mesh,
        in_specs=(P("pair", None, "aux", None), P("pair", None, None), P("pair", None), P(), P()),
        out_specs=P("pair", None, None),
        check_vma=False,
    )
```

time: 431 us -> 55.4 us (0.13)
  waiting for transfers between devices: 126 us -> 0 us
  local copies, waits for them, and re-layouts: 115 us -> 4.98 us
  other arithmetic: 94.1 us -> 0 us
  matrix products: 55 us -> 0 us
  Pallas kernels: 0 us -> 50.2 us
  starting transfers between devices: 24.6 us -> 0 us
  between operations: 13.6 us -> 0.01 us
    gather x33 -> x0, local copies, waits for them, and re-layouts: 100 us -> none  [the longest x8 45.1 us: group_step(): left_block = jnp.take(near_blocks, index_a, axis=0)]
    ppermute x8 -> x0, waiting for transfers between devices: 87.1 us -> none  [shifted(): return lax.ppermute(shard, axis, pairs)]
    select_n x26 -> x0, other arithmetic: 75.9 us -> none  [the longest x8 37.8 us: group_step(): left_block = jnp.take(near_blocks, index_a, axis=0)]
    dot_general x24 -> x0, matrix products: 55 us -> none  [the longest x8 50.1 us: group_step(): jnp.einsum('giPk,gjPk->gij', left_block, matched, preferred_element_type=...]
    pallas_call x0 -> x1, Pallas kernels: none -> 50.2 us  [local(): pl.pallas_call(kernel, out_shape=jax.ShapeDtypeStruct(trials.shape, f32),...]
    psum x1 -> x0, waiting for transfers between devices: 38.5 us -> none  [local(): return lax.psum(result, 'aux')]
    ppermute x8 -> x0, starting transfers between devices: 24.6 us -> none  [shifted(): return lax.ppermute(shard, axis, pairs)]
    scatter-add x16 -> x0, other arithmetic: 16.5 us -> none  [the longest x8 8.24 us: group_step(): return partial_value.at[index_b].add(to_right * keep[:, None, None])]
  transfers between devices with their start and end apart: 9 -> 0, of which waited for: 5 -> 0; matrix products, arithmetic and copies ran while one was open for 1% -> 0% of each run, Pallas kernels for 0% -> 0%
where the time goes in v1:
time: 55.4 us; the launch traced here: 55.2 us
  Pallas kernels  50.2 us (91%)
  local copies, waits for them, and re-layouts  4.98 us (9%)
    pallas_call x1, Pallas kernels, local(): pl.pallas_call(kernel, out_shape=jax.ShapeDtypeStruct(trials.shape, f32),...  50.2 us
    unnamed x12, local copies, waits for them, and re-layouts  4.98 us

profile of v1, /device:TPU:1, one launch (start us, length us, event | category | flops | bytes accessed | tf_op | source)
XLA Modules:
  0.0 55.2 jit_solution(5548141832304370194)
XLA Ops:
  0.0 0.0 copy-start.4
  0.0 0.7 %copy-done.4 = s32[64,2]{0,1:T(2,128)S(1)} copy-done((s32[64,2]{0,1:T(2,128)S(1)}, s32[64,2]{0,1:T(2,128)}, u32[]{:S(2)}) %copy-start.4) | copy-done | bytes 536
  0.7 0.0 copy-start.3
  0.7 0.1 copy.6.pt_ref
  0.8 0.6 %copy-done.3 = s32[256]{0:T(256)S(1)} copy-done((s32[256]{0:T(256)S(1)}, s32[256]{0:T(256)}, u32[]{:S(2)}) %copy-start.3) | copy-done | bytes 1048
  1.4 0.0 copy-start
  1.4 1.2 %copy-done = bf16[2,128,16,128]{3,2,1,0:T(8,128)(2,1)S(1)} copy-done((bf16[2,128,16,128]{3,2,1,0:T(8,128)(2,1)S(1)}, bf16[2,128,16,128]{3,2,1,0:T(8,128)(2,1)}, u32[]{:S(2)}) %copy-start) | copy-done | bytes 1048600
  2.6 0.0 copy-start.1
  2.6 0.9 %copy-done.1 = s32[256,128]{1,0:T(8,128)S(1)} copy-done((s32[256,128]{1,0:T(8,128)S(1)}, s32[256,128]{1,0:T(8,128)}, u32[]{:S(2)}) %copy-start.1) | copy-done | bytes 131096
  3.5 0.0 copy-start.2
  3.5 0.8 %copy-done.2 = bf16[2,128,128]{2,1,0:T(8,128)(2,1)S(1)} copy-done((bf16[2,128,128]{2,1,0:T(8,128)(2,1)S(1)}, bf16[2,128,128]{2,1,0:T(8,128)(2,1)}, u32[]{:S(2)}) %copy-start.2) | copy-done | bytes 65560
  4.3 50.2 %exchange.1 = f32[2,128,128]{2,1,0:T(8,128)S(1)} custom-call(bf16[2,2048,128]{2,1,0:T(8,128)(2,1)S(1)} %bitcast.2, bf16[2,128,128]{2,1,0:T(8,128)(2,1)S(1)} %copy-done.2, s32[64,2]{1,0:T(8,128)S(1)} %copy.6.pt_ref, s32[1,256]{1,0:T(1,128)S(1)} %bitcast.3, s32[256,128]{1,0:T(8,128)S(1)} %copy-done.1), custom_call_target="tpu_custom_call" | custom-call | tf_op jit(solution)/shard_map/exchange/pallas_call | solution.py:269
  54.5 0.7 %copy.8 = f32[2,128,128]{2,1,0:T(8,128)} copy(f32[2,128,128]{2,1,0:T(8,128)S(1)} %exchange.1) | data formatting | bytes 262144
Async XLA Ops:
  0.0 0.7 %copy-start.4 = (s32[64,2]{0,1:T(2,128)S(1)}, s32[64,2]{0,1:T(2,128)}, u32[]{:S(2)}) copy-start(s32[64,2]{0,1:T(2,128)} %param.7) | copy-start | bytes 1540
  0.7 0.7 %copy-start.3 = (s32[256]{0:T(256)S(1)}, s32[256]{0:T(256)}, u32[]{:S(2)}) copy-start(s32[256]{0:T(256)} %param.8) | copy-start | bytes 3076
  1.4 1.2 %copy-start = (bf16[2,128,16,128]{3,2,1,0:T(8,128)(2,1)S(1)}, bf16[2,128,16,128]{3,2,1,0:T(8,128)(2,1)}, u32[]{:S(2)}) copy-start(bf16[2,128,16,128]{3,2,1,0:T(8,128)(2,1)} %param.5) | copy-start | bytes 3145732
  2.6 0.9 %copy-start.1 = (s32[256,128]{1,0:T(8,128)S(1)}, s32[256,128]{1,0:T(8,128)}, u32[]{:S(2)}) copy-start(s32[256,128]{1,0:T(8,128)} %dom_ref.1) | copy-start | bytes 393220
  3.5 0.8 %copy-start.2 = (bf16[2,128,128]{2,1,0:T(8,128)(2,1)S(1)}, bf16[2,128,128]{2,1,0:T(8,128)(2,1)}, u32[]{:S(2)}) copy-start(bf16[2,128,128]{2,1,0:T(8,128)(2,1)} %v_hbm.1) | copy-start | bytes 196612

commit v2 on v1

v2 whole, which is shorter than its diff:
```python
import jax
import jax.numpy as jnp
from jax import lax
from jax.experimental import pallas as pl
from jax.experimental.pallas import tpu as pltpu
from jax.sharding import PartitionSpec as P

MESH = pl.DeviceIdType.MESH
BS = 128
BLK = 2
PLANE = 16
PLANES = 8
AUXW = 16
HALO = 4
SPAN = 2 * HALO + 1
WIN = PLANE + 2 * HALO
SLOTS = WIN * BLK
EDGE = 2 * HALO * BLK
SIDE = 4
MSG = BLK * BS
DEPTH = SPAN * MSG
ORDER = ((2, 2), (1, 2), (2, 1), (2, 3), (3, 2), (0, 2), (1, 1), (1, 3),
         (2, 0), (3, 1), (3, 3), (0, 1), (0, 3), (1, 0), (3, 0))
TURNS = (2, 1, 3, 0)


def dot(a, b, dims=((1,), (0,))):
    return lax.dot_general(a, b, (dims, ((), ())), preferred_element_type=jnp.float32)


def kernel(b_hbm, v_hbm, pt_hbm, slot_hbm, dom_hbm, out_ref,
           braw, vloc, ptv, slotv, domv, bf32, bt, ysend, yw, cntsend, cnt, nown, nz, nx, domax, dombx, mall,
           wsend, wr, acc, other,
           load_sem, own_sem, cs_sem, cr_sem, ns_sem, nr_sem, ys_sem, yr_sem, zs_sem, zr_sem,
           ws_sem, wr_sem, os_sem, or_sem):
    me = lax.axis_index("pair")
    core = lax.axis_index("aux")
    z = me // PLANE
    g = me % PLANE
    x = g // SIDE
    y = g % SIDE
    base = z * PLANE
    up = ((z + 1) % PLANES) * PLANE + g
    down = ((z + PLANES - 1) % PLANES) * PLANE + g
    slot_base = base * BLK - HALO * BLK

    def moved(d):
        return ((x + d[0]) % SIDE) * SIDE + (y + d[1]) % SIDE

    def source(d):
        return ((x + SIDE - d[0]) % SIDE) * SIDE + (y + SIDE - d[1]) % SIDE

    loads = [pltpu.make_async_copy(a, b, load_sem.at[i]) for i, (a, b) in enumerate(
        ((v_hbm, vloc), (b_hbm, braw), (pt_hbm, ptv), (slot_hbm, slotv), (dom_hbm, domv)))]
    for copy in loads:
        copy.start()

    barrier = pltpu.get_barrier_semaphore()
    for d in ORDER:
        pl.semaphore_signal(barrier, inc=1, device_id=(base + moved(d), core), device_id_type=MESH)
    pl.semaphore_signal(barrier, inc=1, device_id=(up, core), device_id_type=MESH)
    pl.semaphore_signal(barrier, inc=1, device_id=(down, core), device_id_type=MESH)
    pl.semaphore_signal(barrier, inc=1, device_id=(me, 1 - core), device_id_type=MESH)

    for copy in loads:
        copy.wait()

    slot_row = slotv[...]
    blocks = slot_row.shape[1]
    pt = ptv[...]
    numbers = lax.broadcasted_iota(jnp.int32, (blocks, pt.shape[1]), 0)
    named_a = (numbers == pt[0:1]).astype(jnp.float32).astype(jnp.bfloat16)
    named_b = (numbers == pt[1:2]).astype(jnp.float32).astype(jnp.bfloat16)
    keep = (pt[0:1] != pt[1:2]).astype(jnp.float32)

    def pick(rows, first):
        wanted = lax.broadcasted_iota(jnp.int32, (rows, blocks), 0) + first
        return (wanted == slot_row).astype(jnp.float32).astype(jnp.bfloat16)

    pick_plane = pick(128, slot_base)
    pick_own = pick(16, (me - HALO // 2) * BLK)
    rows_a = dot(pick_own, named_a).astype(jnp.bfloat16)
    rows_b = (dot(pick_own, named_b) * keep).astype(jnp.bfloat16)
    cols_a = dot(pick_plane, named_a).astype(jnp.bfloat16)
    cols_b = dot(pick_plane, named_b).astype(jnp.bfloat16)
    counts = dot(rows_a, cols_b, ((1,), (1,))) + dot(rows_b, cols_a, ((1,), (1,)))
    cntsend[...] = counts.astype(jnp.bfloat16)
    cnt[g] = counts.astype(jnp.bfloat16)

    for k in range(BLK):
        bf32[...] = braw[k].astype(jnp.float32)
        for p in range(AUXW):
            part = bf32[pl.ds(p, BS, stride=AUXW), :].astype(jnp.bfloat16)
            bt[k, p] = part
            ysend[p, k * BS:(k + 1) * BS, :] = dot(part, vloc[k], ((0,), (0,))).astype(jnp.bfloat16)
    own_y = pltpu.make_async_copy(ysend.at[g], yw.at[pl.ds((HALO + g) * MSG, MSG)], own_sem.at[0])
    own_y.start()

    pl.semaphore_wait(barrier, PLANE + 2)

    def count_copy(to, row):
        return pltpu.make_async_remote_copy(
            cntsend, cnt.at[row], cs_sem.at[to], cr_sem.at[row],
            device_id=(base + to, core), device_id_type=MESH)

    def y_copy(to, row):
        return pltpu.make_async_remote_copy(
            ysend.at[to], yw.at[pl.ds((HALO + row) * MSG, MSG)], ys_sem.at[to], yr_sem.at[row],
            device_id=(base + to, core), device_id_type=MESH)

    def loop(lower, upper, body):
        def step(d, carry):
            body(d)
            return carry
        lax.fori_loop(lower, upper, step, 0)

    for d in ORDER:
        count_copy(moved(d), g).start()
    for d in ORDER:
        y_copy(moved(d), g).start()

    dom = domv[...]
    dom_high = (dom // 128).astype(jnp.float32).astype(jnp.bfloat16)
    dom_low = (dom % 128).astype(jnp.float32).astype(jnp.bfloat16)
    dom_win = dot(pick_plane, dom_high) * 128.0 + dot(pick_plane, dom_low)
    dom_t = dom_win.T
    for a in range(PLANE * BLK):
        column = dom_t[:, HALO * BLK + a:HALO * BLK + a + 1]
        domax[a] = jnp.broadcast_to(column, (128, 128)).astype(jnp.int32).astype(jnp.int16)
    for s in range(SLOTS):
        dombx[s] = jnp.broadcast_to(dom_win[s:s + 1], (16, 128)).astype(jnp.int32).astype(jnp.int16)

    for d in ORDER:
        count_copy(moved(d), source(d)).wait_recv()
    place_row = lax.broadcasted_iota(jnp.int32, (SLOTS, PLANE * 16), 0)
    place_col = lax.broadcasted_iota(jnp.int32, (SLOTS, PLANE * 16), 1)
    place = (place_row == BLK * (place_col // 16 + HALO // 2) + place_col % 16)
    total = dot(place.astype(jnp.float32).astype(jnp.bfloat16), cnt[...].reshape(PLANE * 16, 128))
    nown[...] = total
    n_up = pltpu.make_async_remote_copy(nown.at[pl.ds(SLOTS - EDGE, EDGE)], nz.at[0], ns_sem.at[0], nr_sem.at[0],
                                        device_id=(up, core), device_id_type=MESH)
    n_down = pltpu.make_async_remote_copy(nown.at[pl.ds(0, EDGE)], nz.at[1], ns_sem.at[1], nr_sem.at[1],
                                          device_id=(down, core), device_id_type=MESH)
    n_up.start()
    n_down.start()

    def spread(matrix):
        for s in range(SLOTS):
            nx[s] = jnp.broadcast_to(matrix[HALO * BLK:HALO * BLK + PLANE * BLK, s:s + 1], (PLANE * BLK, 128))

    def build(i):
        for k in range(BLK):
            a = i * BLK + k
            left = domax[a]
            for s in range(SPAN * BLK):
                weight = jnp.broadcast_to(nx[i * BLK + s, pl.ds(a, 1), :], (16, 128)).astype(jnp.bfloat16)
                right = dombx[i * BLK + s]
                for h in range(BS // 16):
                    tile = jnp.where(left[h * 16:(h + 1) * 16] == right, weight, jnp.bfloat16(0))
                    mall[i, k * BS + h * 16:k * BS + (h + 1) * 16, s * BS:(s + 1) * BS] = tile

    spread(total)
    loop(HALO, PLANE - HALO, build)

    n_up.wait()
    n_down.wait()
    shift = PLANE * BLK
    lanes = lax.broadcasted_iota(jnp.int32, (EDGE, 128), 1)
    from_low = jnp.where(lanes < EDGE, pltpu.roll(nz[0], 128 - shift, 1), 0.0)
    from_high = jnp.where((lanes >= shift) & (lanes < SLOTS), pltpu.roll(nz[1], shift, 1), 0.0)
    total = total + jnp.concatenate([from_low, jnp.zeros((SLOTS - 2 * EDGE, 128), jnp.float32), from_high], axis=0)
    spread(total)
    loop(0, HALO, build)
    loop(PLANE - HALO, PLANE, build)

    def z_copy(upward, n):
        row = (PLANE if upward else HALO) + n
        to = n if upward else HALO + PLANE + n
        side = 0 if upward else 1
        return pltpu.make_async_remote_copy(
            yw.at[pl.ds(row * MSG, MSG)], yw.at[pl.ds(to * MSG, MSG)],
            zs_sem.at[side, n], zr_sem.at[side, n],
            device_id=(up if upward else down, core), device_id_type=MESH)

    def relay(row):
        @pl.when(row >= PLANE - HALO)
        def _():
            z_copy(True, row - (PLANE - HALO)).start()

        @pl.when(row < HALO)
        def _():
            z_copy(False, row).start()

    own_y.wait()
    relay(g)
    for d in ORDER:
        y_copy(moved(d), source(d)).wait_recv()
        relay(source(d))

    def w_copy(i, row):
        return pltpu.make_async_remote_copy(
            wsend.at[i], wr.at[row], ws_sem.at[i], wr_sem.at[row],
            device_id=(base + i, core), device_id_type=MESH)

    def apply_index(i):
        w = dot(mall[i], yw[pl.ds(i * MSG, DEPTH), :]).astype(jnp.bfloat16)
        wsend[i] = w

        @pl.when(i != g)
        def _():
            w_copy(i, g).start()

    side = x // 2

    def turn(t):
        return sum(jnp.where(t == n, TURNS[n], 0) for n in range(SIDE))

    def inner(t):
        row = 2 - side + (t // SIDE) * (2 * side - 1)
        apply_index(row * SIDE + (y + turn(t % SIDE)) % SIDE)

    def outer(t):
        row = 3 - 3 * side + (t // SIDE) * (6 * side - 3)
        apply_index(row * SIDE + (y + turn(t % SIDE)) % SIDE)

    loop(0, 2 * SIDE, inner)
    for n in range(HALO):
        z_copy(True, n).wait()
        z_copy(False, n).wait()
    loop(0, 2 * SIDE, outer)

    def add(row):
        for k in range(BLK):
            acc[k] += dot(bt[k, row], wr[row, k * BS:(k + 1) * BS, :])

    own_w = pltpu.make_async_copy(wsend.at[g], wr.at[g], own_sem.at[1])
    own_w.start()
    acc[...] = jnp.zeros_like(acc)
    own_w.wait()
    add(g)

    def collect(t):
        sender = (2 * (1 - side) + 2 * (t // 8) + t % 2) % SIDE
        row = sender * SIDE + (y + SIDE - turn((t % 8) // 2)) % SIDE

        @pl.when(row != g)
        def _():
            w_copy(row, row).wait_recv()
            add(row)

    loop(0, PLANE, collect)

    swap = pltpu.make_async_remote_copy(acc, other, os_sem, or_sem,
                                        device_id=(me, 1 - core), device_id_type=MESH)
    swap.start()

    for d in ORDER:
        count_copy(moved(d), g).wait_send()
        y_copy(moved(d), g).wait_send()
        w_copy(moved(d), g).wait_send()
    swap.wait()
    out_ref[...] = acc[...] + other[...]


def local(half_transformed, trials, pair_table, block_slot, domains):
    blocks = half_transformed.shape[0]
    count = block_slot.shape[0]
    vmem = pl.BlockSpec(memory_space=pltpu.VMEM)
    hbm = pl.BlockSpec(memory_space=pl.ANY)
    bf, f32 = jnp.bfloat16, jnp.float32
    dma = pltpu.SemaphoreType.DMA
    scratch = [
        pltpu.VMEM((BLK, BS * AUXW, 128), bf),
        pltpu.VMEM((BLK, BS, 128), bf),
        pltpu.VMEM((2, pair_table.shape[0]), jnp.int32),
        pltpu.VMEM((1, count), jnp.int32),
        pltpu.VMEM((count, 128), jnp.int32),
        pltpu.VMEM((BS * AUXW, 128), f32),
        pltpu.VMEM((BLK, AUXW, BS, 128), bf),
        pltpu.VMEM((AUXW, MSG, 128), bf),
        pltpu.VMEM((WIN * MSG, 128), bf),
        pltpu.VMEM((16, 128), bf),
        pltpu.VMEM((PLANE, 16, 128), bf),
        pltpu.VMEM((SLOTS, 128), f32),
        pltpu.VMEM((2, EDGE, 128), f32),
        pltpu.VMEM((SLOTS, PLANE * BLK, 128), f32),
        pltpu.VMEM((PLANE * BLK, 128, 128), jnp.int16),
        pltpu.VMEM((SLOTS, 16, 128), jnp.int16),
        pltpu.VMEM((PLANE, MSG, DEPTH), bf),
        pltpu.VMEM((PLANE, MSG, 128), bf),
        pltpu.VMEM((AUXW, MSG, 128), bf),
        pltpu.VMEM((BLK, BS, 128), f32),
        pltpu.VMEM((BLK, BS, 128), f32),
        dma((5,)), dma((2,)), dma((PLANE,)), dma((PLANE,)), dma((2,)), dma((2,)),
        dma((PLANE,)), dma((PLANE,)), dma((2, HALO)), dma((2, HALO)), dma((PLANE,)), dma((PLANE,)), dma, dma,
    ]
    return pl.pallas_call(
        kernel,
        out_shape=jax.ShapeDtypeStruct(trials.shape, f32),
        in_specs=[hbm] * 5,
        out_specs=vmem,
        scratch_shapes=scratch,
        compiler_params=pltpu.CompilerParams(collective_id=1, has_side_effects=True, vmem_limit_bytes=62 << 20),
        name="exchange",
    )(half_transformed.reshape(blocks, BS * AUXW, 128), trials, pair_table.T,
      block_slot.reshape(1, -1), domains)


def solution(mesh):
    return jax.shard_map(
        local,
        mesh=mesh,
        in_specs=(P("pair", None, "aux", None), P("pair", None, None), P("pair", None), P(), P()),
        out_specs=P("pair", None, None),
        check_vma=False,
    )
```

time: 55.4 us -> 49.1 us (0.89)
  local copies, waits for them, and re-layouts: 4.98 us -> 1.57 us
  Pallas kernels: 50.2 us -> 47.4 us
    unnamed x12 -> x1, local copies, waits for them, and re-layouts: 4.98 us -> 1.57 us
    pallas_call x1, Pallas kernels: 50.2 us -> 47.4 us  [local(): pl.pallas_call(kernel, out_shape=jax.ShapeDtypeStruct(trials.shape, f32),...]
where the time goes in v2:
time: 49.1 us; the launch traced here: 49 us
  Pallas kernels  47.4 us (97%)
  local copies, waits for them, and re-layouts  1.57 us (3%)
    pallas_call x1, Pallas kernels, local(): pl.pallas_call(kernel, out_shape=jax.ShapeDtypeStruct(trials.shape, f32),...  47.4 us
    unnamed x1, local copies, waits for them, and re-layouts  1.57 us

profile of v2, /device:TPU:1, one launch (start us, length us, event | category | flops | bytes accessed | tf_op | source)
XLA Modules:
  0.0 49.0 jit_solution(3946038498743867024)
XLA Ops:
  0.0 47.4 %exchange.1 = f32[2,128,128]{2,1,0:T(8,128)} custom-call(bf16[2,2048,128]{2,1,0:T(8,128)(2,1)} %bitcast.3, bf16[2,128,128]{2,1,0:T(8,128)(2,1)} %v_hbm.1, s32[2,64]{1,0:T(2,128)} %bitcast.4, s32[1,256]{1,0:T(1,128)} %bitcast.5, s32[256,128]{1,0:T(8,128)} %dom_hbm.1), custom_call_target="tpu_custom_call" | custom-call | tf_op jit(solution)/shard_map/exchange/pallas_call | solution.py:297
  47.4 1.6 %copy.7 = f32[2,128,128]{2,1,0:T(8,128)} copy(f32[2,128,128]{2,1,0:T(8,128)} %exchange.1) | data formatting | bytes 262144

commit v3 on v2

--- a/solution.py
+++ b/solution.py
@@ -18,6 +18,7 @@
 EDGE = 2 * HALO * BLK
 SIDE = 4
 MSG = BLK * BS
+OWN = (HALO + 1) * BLK
 DEPTH = SPAN * MSG
 ORDER = ((2, 2), (1, 2), (2, 1), (2, 3), (3, 2), (0, 2), (1, 1), (1, 3),
          (2, 0), (3, 1), (3, 3), (0, 1), (0, 3), (1, 0), (3, 0))
@@ -28,9 +29,19 @@
     return lax.dot_general(a, b, (dims, ((), ())), preferred_element_type=jnp.float32)
 
 
+def ceil_log2(value):
+    return jnp.ceil(jnp.log(value) * 1.4426950408889634)
+
+
+def halves(value):
+    high = value.astype(jnp.bfloat16)
+    low = (value - high.astype(jnp.float32)).astype(jnp.bfloat16)
+    return jnp.concatenate([high, low], axis=1)
+
+
 def kernel(b_hbm, v_hbm, pt_hbm, slot_hbm, dom_hbm, out_ref,
-           braw, vloc, ptv, slotv, domv, bf32, bt, ysend, yw, cntsend, cnt, nown, nz, nx, domax, dombx, mall,
-           wsend, wr, acc, other,
+           braw, vloc, ptv, slotv, domv, bf32, bt, yf32, ysend, yraw, yw, yunit, wpower, cntsend, cnt, nsend, nz, nx, domax, dombx, mall,
+           wsend, wr, wfull, acc, other,
            load_sem, own_sem, cs_sem, cr_sem, ns_sem, nr_sem, ys_sem, yr_sem, zs_sem, zr_sem,
            ws_sem, wr_sem, os_sem, or_sem):
     me = lax.axis_index("pair")
@@ -84,16 +95,26 @@
     cols_a = dot(pick_plane, named_a).astype(jnp.bfloat16)
     cols_b = dot(pick_plane, named_b).astype(jnp.bfloat16)
     counts = dot(rows_a, cols_b, ((1,), (1,))) + dot(rows_b, cols_a, ((1,), (1,)))
+    marks = []
+    for k in range(BLK):
+        bf32[k] = braw[k].astype(jnp.float32)
+        top = jnp.full((8, 128), 1e-30, jnp.float32)
+        for p in range(AUXW):
+            part = bf32[k, pl.ds(p, BS, stride=AUXW), :].astype(jnp.bfloat16)
+            bt[k, :, p * BS:(p + 1) * BS] = part
+            value = dot(part, vloc[k], ((0,), (0,)))
+            yf32[p, k * BS:(k + 1) * BS, :] = value
+            top = jnp.maximum(top, jnp.max(jnp.abs(value).reshape(BS // 8, 8, 128), axis=0))
+        power = ceil_log2(jnp.max(top, axis=0, keepdims=True) * (1.0 / 32000.0))
+        unit = jnp.exp2(-power)
+        for p in range(AUXW):
+            ysend[p, k * BS:(k + 1) * BS, :] = jnp.round(yf32[p, k * BS:(k + 1) * BS, :] * unit).astype(jnp.int16)
+        marks.append(power)
+    own_row = lax.broadcasted_iota(jnp.int32, (16, 128), 0)
+    counts = jnp.where(own_row == OWN, marks[0], jnp.where(own_row == OWN + 1, marks[1], counts))
     cntsend[...] = counts.astype(jnp.bfloat16)
     cnt[g] = counts.astype(jnp.bfloat16)
-
-    for k in range(BLK):
-        bf32[...] = braw[k].astype(jnp.float32)
-        for p in range(AUXW):
-            part = bf32[pl.ds(p, BS, stride=AUXW), :].astype(jnp.bfloat16)
-            bt[k, p] = part
-            ysend[p, k * BS:(k + 1) * BS, :] = dot(part, vloc[k], ((0,), (0,))).astype(jnp.bfloat16)
-    own_y = pltpu.make_async_copy(ysend.at[g], yw.at[pl.ds((HALO + g) * MSG, MSG)], own_sem.at[0])
+    own_y = pltpu.make_async_copy(ysend.at[g], yraw.at[HALO + g], own_sem.at[0])
     own_y.start()
 
     pl.semaphore_wait(barrier, PLANE + 2)
@@ -105,7 +126,7 @@
 
     def y_copy(to, row):
         return pltpu.make_async_remote_copy(
-            ysend.at[to], yw.at[pl.ds((HALO + row) * MSG, MSG)], ys_sem.at[to], yr_sem.at[row],
+            ysend.at[to], yraw.at[HALO + row], ys_sem.at[to], yr_sem.at[row],
             device_id=(base + to, core), device_id_type=MESH)
 
     def loop(lower, upper, body):
@@ -134,29 +155,38 @@
         count_copy(moved(d), source(d)).wait_recv()
     place_row = lax.broadcasted_iota(jnp.int32, (SLOTS, PLANE * 16), 0)
     place_col = lax.broadcasted_iota(jnp.int32, (SLOTS, PLANE * 16), 1)
-    place = (place_row == BLK * (place_col // 16 + HALO // 2) + place_col % 16)
-    total = dot(place.astype(jnp.float32).astype(jnp.bfloat16), cnt[...].reshape(PLANE * 16, 128))
-    nown[...] = total
-    n_up = pltpu.make_async_remote_copy(nown.at[pl.ds(SLOTS - EDGE, EDGE)], nz.at[0], ns_sem.at[0], nr_sem.at[0],
+    place_own = place_col % 16
+    place = (place_row == BLK * (place_col // 16 + HALO // 2) + place_own) & (place_own < OWN)
+    place_power = (place_row == BLK * (place_col // 16 + HALO) + place_own - OWN) & (place_own >= OWN) & (place_own < OWN + BLK)
+    messages = cnt[...].reshape(PLANE * 16, 128)
+    total = dot(place.astype(jnp.float32).astype(jnp.bfloat16), messages)
+    power = dot(place_power.astype(jnp.float32).astype(jnp.bfloat16), messages)
+    nsend[0] = jnp.concatenate([total[SLOTS - EDGE:], power[SLOTS - EDGE:SLOTS - EDGE // 2]], axis=0)
+    nsend[1] = jnp.concatenate([total[:EDGE], power[EDGE // 2:EDGE]], axis=0)
+    n_up = pltpu.make_async_remote_copy(nsend.at[0], nz.at[0], ns_sem.at[0], nr_sem.at[0],
                                         device_id=(up, core), device_id_type=MESH)
-    n_down = pltpu.make_async_remote_copy(nown.at[pl.ds(0, EDGE)], nz.at[1], ns_sem.at[1], nr_sem.at[1],
+    n_down = pltpu.make_async_remote_copy(nsend.at[1], nz.at[1], ns_sem.at[1], nr_sem.at[1],
                                           device_id=(down, core), device_id_type=MESH)
     n_up.start()
     n_down.start()
 
     def spread(matrix):
-        for s in range(SLOTS):
-            nx[s] = jnp.broadcast_to(matrix[HALO * BLK:HALO * BLK + PLANE * BLK, s:s + 1], (PLANE * BLK, 128))
+        rows = matrix[HALO * BLK:HALO * BLK + PLANE * BLK]
+        half = jnp.where(rows > 256.0, 0.5, 0.0)
+        for n, side_of in enumerate((rows - half, rows + half)):
+            for s in range(SLOTS):
+                nx[n, s] = jnp.broadcast_to(side_of[:, s:s + 1], (PLANE * BLK, 128))
 
     def build(i):
         for k in range(BLK):
             a = i * BLK + k
             left = domax[a]
             for s in range(SPAN * BLK):
-                weight = jnp.broadcast_to(nx[i * BLK + s, pl.ds(a, 1), :], (16, 128)).astype(jnp.bfloat16)
+                weight = [jnp.broadcast_to(nx[n, i * BLK + s, pl.ds(a, 1), :], (16, 128)).astype(jnp.bfloat16)
+                          for n in range(2)]
                 right = dombx[i * BLK + s]
                 for h in range(BS // 16):
-                    tile = jnp.where(left[h * 16:(h + 1) * 16] == right, weight, jnp.bfloat16(0))
+                    tile = jnp.where(left[h * 16:(h + 1) * 16] == right, weight[h % 2], jnp.bfloat16(0))
                     mall[i, k * BS + h * 16:k * BS + (h + 1) * 16, s * BS:(s + 1) * BS] = tile
 
     spread(total)
@@ -166,10 +196,16 @@
     n_down.wait()
     shift = PLANE * BLK
     lanes = lax.broadcasted_iota(jnp.int32, (EDGE, 128), 1)
-    from_low = jnp.where(lanes < EDGE, pltpu.roll(nz[0], 128 - shift, 1), 0.0)
-    from_high = jnp.where((lanes >= shift) & (lanes < SLOTS), pltpu.roll(nz[1], shift, 1), 0.0)
+    from_low = jnp.where(lanes < EDGE, pltpu.roll(nz[0, :EDGE], 128 - shift, 1), 0.0)
+    from_high = jnp.where((lanes >= shift) & (lanes < SLOTS), pltpu.roll(nz[1, :EDGE], shift, 1), 0.0)
     total = total + jnp.concatenate([from_low, jnp.zeros((SLOTS - 2 * EDGE, 128), jnp.float32), from_high], axis=0)
     spread(total)
+    power = jnp.concatenate([nz[0, EDGE:], power[EDGE // 2:SLOTS - EDGE // 2], nz[1, EDGE:]], axis=0)
+    units = jnp.exp2(power)
+    yunit[...] = units
+    units = jnp.concatenate([units, jnp.zeros((128 - SLOTS, 128), jnp.float32)], axis=0).astype(jnp.bfloat16)
+    bound = dot(total[HALO * BLK:HALO * BLK + PLANE * BLK].astype(jnp.bfloat16), units)
+    wpower[...] = ceil_log2(jnp.maximum(bound, 1e-35) * 1.001)
     loop(0, HALO, build)
     loop(PLANE - HALO, PLANE, build)
 
@@ -178,7 +214,7 @@
         to = n if upward else HALO + PLANE + n
         side = 0 if upward else 1
         return pltpu.make_async_remote_copy(
-            yw.at[pl.ds(row * MSG, MSG)], yw.at[pl.ds(to * MSG, MSG)],
+            yraw.at[row], yraw.at[to],
             zs_sem.at[side, n], zr_sem.at[side, n],
             device_id=(up if upward else down, core), device_id_type=MESH)
 
@@ -191,11 +227,26 @@
         def _():
             z_copy(False, row).start()
 
+    def unpack(w):
+        for k in range(BLK):
+            value = yraw[w, k * BS:(k + 1) * BS, :].astype(jnp.float32) * yunit[pl.ds(w * BLK + k, 1), :]
+            yw[pl.ds(w * MSG + k * BS, BS), :] = halves(value)
+
+    def step(t):
+        code = sum(jnp.where(t == n, SIDE * d[0] + d[1], 0) for n, d in enumerate(ORDER))
+        return code // SIDE, code % SIDE
+
     own_y.wait()
     relay(g)
-    for d in ORDER:
-        y_copy(moved(d), source(d)).wait_recv()
-        relay(source(d))
+    unpack(HALO + g)
+
+    def arrive(t):
+        row = source(step(t))
+        y_copy(row, row).wait_recv()
+        relay(row)
+        unpack(HALO + row)
+
+    loop(0, PLANE - 1, arrive)
 
     def w_copy(i, row):
         return pltpu.make_async_remote_copy(
@@ -203,8 +254,11 @@
             device_id=(base + i, core), device_id_type=MESH)
 
     def apply_index(i):
-        w = dot(mall[i], yw[pl.ds(i * MSG, DEPTH), :]).astype(jnp.bfloat16)
-        wsend[i] = w
+        both = dot(mall[i], yw[pl.ds(i * MSG, DEPTH), :])
+        for k in range(BLK):
+            part = both[k * BS:(k + 1) * BS]
+            unit = jnp.exp2(-wpower[pl.ds(i * BLK + k, 1), :])
+            wsend[i, k * BS:(k + 1) * BS, :] = jnp.round((part[:, :128] + part[:, 128:]) * unit).astype(jnp.int16)
 
         @pl.when(i != g)
         def _():
@@ -227,29 +281,40 @@
     for n in range(HALO):
         z_copy(True, n).wait()
         z_copy(False, n).wait()
+        unpack(n)
+        unpack(HALO + PLANE + n)
     loop(0, 2 * SIDE, outer)
 
-    def add(row):
-        for k in range(BLK):
-            acc[k] += dot(bt[k, row], wr[row, k * BS:(k + 1) * BS, :])
+    def gather(row):
+        for k in range(BLK):
+            wfull[k, pl.ds(row * BS, BS), :] = halves(wr[row, k * BS:(k + 1) * BS, :].astype(jnp.float32))
 
     own_w = pltpu.make_async_copy(wsend.at[g], wr.at[g], own_sem.at[1])
     own_w.start()
-    acc[...] = jnp.zeros_like(acc)
     own_w.wait()
-    add(g)
-
-    def collect(t):
-        sender = (2 * (1 - side) + 2 * (t // 8) + t % 2) % SIDE
-        row = sender * SIDE + (y + SIDE - turn((t % 8) // 2)) % SIDE
+    gather(g)
+
+    def collect(t, first):
+        sender = first + t % 2
+        row = sender * SIDE + (y + SIDE - turn(t // 2)) % SIDE
 
         @pl.when(row != g)
         def _():
             w_copy(row, row).wait_recv()
-            add(row)
-
-    loop(0, PLANE, collect)
-
+            gather(row)
+
+    half = AUXW * BS // 2
+    for n in range(2):
+        first = 2 * ((side + 1 + n) % 2)
+        loop(0, 2 * SIDE, lambda t: collect(t, first))
+        depth = pl.ds(pl.multiple_of(first // 2 * half, half), half)
+        for k in range(BLK):
+            both = dot(bt[k, :, depth], wfull[k, depth, :])
+            part = both[:, :128] + both[:, 128:]
+            acc[k] = part if n == 0 else acc[k] + part
+
+    for k in range(BLK):
+        acc[k] = acc[k] * jnp.exp2(wpower[pl.ds(g * BLK + k, 1), :])
     swap = pltpu.make_async_remote_copy(acc, other, os_sem, or_sem,
                                         device_id=(me, 1 - core), device_id_type=MESH)
     swap.start()
@@ -275,20 +340,25 @@
         pltpu.VMEM((2, pair_table.shape[0]), jnp.int32),
         pltpu.VMEM((1, count), jnp.int32),
         pltpu.VMEM((count, 128), jnp.int32),
-        pltpu.VMEM((BS * AUXW, 128), f32),
-        pltpu.VMEM((BLK, AUXW, BS, 128), bf),
-        pltpu.VMEM((AUXW, MSG, 128), bf),
-        pltpu.VMEM((WIN * MSG, 128), bf),
+        pltpu.VMEM((BLK, BS * AUXW, 128), f32),
+        pltpu.VMEM((BLK, BS, AUXW * 128), bf),
+        pltpu.VMEM((AUXW, MSG, 128), f32),
+        pltpu.VMEM((AUXW, MSG, 128), jnp.int16),
+        pltpu.VMEM((WIN, MSG, 128), jnp.int16),
+        pltpu.VMEM((WIN * MSG, 256), bf),
+        pltpu.VMEM((SLOTS, 128), f32),
+        pltpu.VMEM((PLANE * BLK, 128), f32),
         pltpu.VMEM((16, 128), bf),
         pltpu.VMEM((PLANE, 16, 128), bf),
-        pltpu.VMEM((SLOTS, 128), f32),
-        pltpu.VMEM((2, EDGE, 128), f32),
-        pltpu.VMEM((SLOTS, PLANE * BLK, 128), f32),
+        pltpu.VMEM((2, EDGE + EDGE // 2, 128), f32),
+        pltpu.VMEM((2, EDGE + EDGE // 2, 128), f32),
+        pltpu.VMEM((2, SLOTS, PLANE * BLK, 128), f32),
         pltpu.VMEM((PLANE * BLK, 128, 128), jnp.int16),
         pltpu.VMEM((SLOTS, 16, 128), jnp.int16),
         pltpu.VMEM((PLANE, MSG, DEPTH), bf),
-        pltpu.VMEM((PLANE, MSG, 128), bf),
-        pltpu.VMEM((AUXW, MSG, 128), bf),
+        pltpu.VMEM((PLANE, MSG, 128), jnp.int16),
+        pltpu.VMEM((AUXW, MSG, 128), jnp.int16),
+        pltpu.VMEM((BLK, AUXW * 128, 256), bf),
         pltpu.VMEM((BLK, BS, 128), f32),
         pltpu.VMEM((BLK, BS, 128), f32),
         dma((5,)), dma((2,)), dma((PLANE,)), dma((PLANE,)), dma((2,)), dma((2,)),

time: 49.1 us -> 49.8 us (1.014)
  Pallas kernels: 47.4 us -> 48.1 us
    pallas_call x1, Pallas kernels: 47.4 us -> 48.1 us  [local(): pl.pallas_call(kernel, out_shape=jax.ShapeDtypeStruct(trials.shape, f32),...]
where the time goes in v3:
time: 49.8 us; the launch traced here: 49.7 us
  Pallas kernels  48.1 us (97%)
  local copies, waits for them, and re-layouts  1.57 us (3%)
    pallas_call x1, Pallas kernels, local(): pl.pallas_call(kernel, out_shape=jax.ShapeDtypeStruct(trials.shape, f32),...  48.1 us
    unnamed x1, local copies, waits for them, and re-layouts  1.57 us

profile of v3, /device:TPU:1, one launch (start us, length us, event | category | flops | bytes accessed | tf_op | source)
XLA Modules:
  0.0 49.7 jit_solution(43719404021230381)
XLA Ops:
  0.0 48.1 %exchange.1 = f32[2,128,128]{2,1,0:T(8,128)} custom-call(bf16[2,2048,128]{2,1,0:T(8,128)(2,1)} %bitcast.3, bf16[2,128,128]{2,1,0:T(8,128)(2,1)} %v_hbm.1, s32[2,64]{1,0:T(2,128)} %bitcast.4, s32[1,256]{1,0:T(1,128)} %bitcast.5, s32[256,128]{1,0:T(8,128)} %dom_hbm.1), custom_call_target="tpu_custom_call" | custom-call | tf_op jit(solution)/shard_map/exchange/pallas_call | solution.py:367
  48.1 1.6 %copy.7 = f32[2,128,128]{2,1,0:T(8,128)} copy(f32[2,128,128]{2,1,0:T(8,128)} %exchange.1) | data formatting | bytes 262144

commit v4 on v3

--- a/solution.py
+++ b/solution.py
@@ -62,7 +62,7 @@
         return ((x + SIDE - d[0]) % SIDE) * SIDE + (y + SIDE - d[1]) % SIDE
 
     loads = [pltpu.make_async_copy(a, b, load_sem.at[i]) for i, (a, b) in enumerate(
-        ((v_hbm, vloc), (b_hbm, braw), (pt_hbm, ptv), (slot_hbm, slotv), (dom_hbm, domv)))]
+        ((pt_hbm, ptv), (slot_hbm, slotv), (v_hbm, vloc), (b_hbm, braw), (dom_hbm, domv)))]
     for copy in loads:
         copy.start()
 
@@ -73,8 +73,9 @@
     pl.semaphore_signal(barrier, inc=1, device_id=(down, core), device_id_type=MESH)
     pl.semaphore_signal(barrier, inc=1, device_id=(me, 1 - core), device_id_type=MESH)
 
-    for copy in loads:
-        copy.wait()
+    load_pairs, load_slots, load_v, load_b, load_domains = loads
+    load_pairs.wait()
+    load_slots.wait()
 
     slot_row = slotv[...]
     blocks = slot_row.shape[1]
@@ -95,6 +96,8 @@
     cols_a = dot(pick_plane, named_a).astype(jnp.bfloat16)
     cols_b = dot(pick_plane, named_b).astype(jnp.bfloat16)
     counts = dot(rows_a, cols_b, ((1,), (1,))) + dot(rows_b, cols_a, ((1,), (1,)))
+    load_v.wait()
+    load_b.wait()
     marks = []
     for k in range(BLK):
         bf32[k] = braw[k].astype(jnp.float32)
@@ -140,6 +143,7 @@
     for d in ORDER:
         y_copy(moved(d), g).start()
 
+    load_domains.wait()
     dom = domv[...]
     dom_high = (dom // 128).astype(jnp.float32).astype(jnp.bfloat16)
     dom_low = (dom % 128).astype(jnp.float32).astype(jnp.bfloat16)
@@ -206,8 +210,6 @@
     units = jnp.concatenate([units, jnp.zeros((128 - SLOTS, 128), jnp.float32)], axis=0).astype(jnp.bfloat16)
     bound = dot(total[HALO * BLK:HALO * BLK + PLANE * BLK].astype(jnp.bfloat16), units)
     wpower[...] = ceil_log2(jnp.maximum(bound, 1e-35) * 1.001)
-    loop(0, HALO, build)
-    loop(PLANE - HALO, PLANE, build)
 
     def z_copy(upward, n):
         row = (PLANE if upward else HALO) + n
@@ -246,7 +248,10 @@
         relay(row)
         unpack(HALO + row)
 
-    loop(0, PLANE - 1, arrive)
+    loop(0, 5, arrive)
+    loop(0, HALO, build)
+    loop(PLANE - HALO, PLANE, build)
+    loop(5, PLANE - 1, arrive)
 
     def w_copy(i, row):
         return pltpu.make_async_remote_copy(

time: 49.8 us -> 49.5 us (level)
  no operation moved by 1% of the time
where the time goes in v4:
time: 49.5 us; the launch traced here: 49.4 us
  Pallas kernels  47.8 us (97%)
  local copies, waits for them, and re-layouts  1.57 us (3%)
    pallas_call x1, Pallas kernels, local(): pl.pallas_call(kernel, out_shape=jax.ShapeDtypeStruct(trials.shape, f32),...  47.8 us
    unnamed x1, local copies, waits for them, and re-layouts  1.57 us

profile of v4, /device:TPU:1, one launch (start us, length us, event | category | flops | bytes accessed | tf_op | source)
XLA Modules:
  0.0 49.4 jit_solution(15622673874138160887)
XLA Ops:
  0.0 47.8 %exchange.1 = f32[2,128,128]{2,1,0:T(8,128)} custom-call(bf16[2,2048,128]{2,1,0:T(8,128)(2,1)} %bitcast.3, bf16[2,128,128]{2,1,0:T(8,128)(2,1)} %v_hbm.1, s32[2,64]{1,0:T(2,128)} %bitcast.4, s32[1,256]{1,0:T(1,128)} %bitcast.5, s32[256,128]{1,0:T(8,128)} %dom_hbm.1), custom_call_target="tpu_custom_call" | custom-call | tf_op jit(solution)/shard_map/exchange/pallas_call | solution.py:372
  47.9 1.6 %copy.7 = f32[2,128,128]{2,1,0:T(8,128)} copy(f32[2,128,128]{2,1,0:T(8,128)} %exchange.1) | data formatting | bytes 262144

commit v5 on v4

--- a/solution.py
+++ b/solution.py
@@ -308,6 +308,8 @@
             w_copy(row, row).wait_recv()
             gather(row)
 
+    swaps = [pltpu.make_async_remote_copy(acc.at[k], other.at[k], os_sem.at[k], or_sem.at[k],
+                                          device_id=(me, 1 - core), device_id_type=MESH) for k in range(BLK)]
     half = AUXW * BS // 2
     for n in range(2):
         first = 2 * ((side + 1 + n) % 2)
@@ -316,20 +318,19 @@
         for k in range(BLK):
             both = dot(bt[k, :, depth], wfull[k, depth, :])
             part = both[:, :128] + both[:, 128:]
-            acc[k] = part if n == 0 else acc[k] + part
-
-    for k in range(BLK):
-        acc[k] = acc[k] * jnp.exp2(wpower[pl.ds(g * BLK + k, 1), :])
-    swap = pltpu.make_async_remote_copy(acc, other, os_sem, or_sem,
-                                        device_id=(me, 1 - core), device_id_type=MESH)
-    swap.start()
+            if n == 0:
+                acc[k] = part
+            else:
+                acc[k] = (acc[k] + part) * jnp.exp2(wpower[pl.ds(g * BLK + k, 1), :])
+                swaps[k].start()
 
     for d in ORDER:
         count_copy(moved(d), g).wait_send()
         y_copy(moved(d), g).wait_send()
         w_copy(moved(d), g).wait_send()
-    swap.wait()
-    out_ref[...] = acc[...] + other[...]
+    for k in range(BLK):
+        swaps[k].wait()
+        out_ref[k] = acc[k] + other[k]
 
 
 def local(half_transformed, trials, pair_table, block_slot, domains):
@@ -367,7 +368,7 @@
         pltpu.VMEM((BLK, BS, 128), f32),
         pltpu.VMEM((BLK, BS, 128), f32),
         dma((5,)), dma((2,)), dma((PLANE,)), dma((PLANE,)), dma((2,)), dma((2,)),
-        dma((PLANE,)), dma((PLANE,)), dma((2, HALO)), dma((2, HALO)), dma((PLANE,)), dma((PLANE,)), dma, dma,
+        dma((PLANE,)), dma((PLANE,)), dma((2, HALO)), dma((2, HALO)), dma((PLANE,)), dma((PLANE,)), dma((BLK,)), dma((BLK,)),
     ]
     return pl.pallas_call(
         kernel,

time: 49.5 us -> 49.7 us (level)
  no operation moved by 1% of the time
where the time goes in v5:
time: 49.7 us; the launch traced here: 49.6 us
  Pallas kernels  48 us (97%)
  local copies, waits for them, and re-layouts  1.57 us (3%)
    pallas_call x1, Pallas kernels, local(): pl.pallas_call(kernel, out_shape=jax.ShapeDtypeStruct(trials.shape, f32),...  48 us
    unnamed x1, local copies, waits for them, and re-layouts  1.57 us

profile of v5, /device:TPU:1, one launch (start us, length us, event | category | flops | bytes accessed | tf_op | source)
XLA Modules:
  0.0 49.6 jit_solution(5821196109235314676)
XLA Ops:
  0.0 48.0 %exchange.1 = f32[2,128,128]{2,1,0:T(8,128)} custom-call(bf16[2,2048,128]{2,1,0:T(8,128)(2,1)} %bitcast.3, bf16[2,128,128]{2,1,0:T(8,128)(2,1)} %v_hbm.1, s32[2,64]{1,0:T(2,128)} %bitcast.4, s32[1,256]{1,0:T(1,128)} %bitcast.5, s32[256,128]{1,0:T(8,128)} %dom_hbm.1), custom_call_target="tpu_custom_call" | custom-call | tf_op jit(solution)/shard_map/exchange/pallas_call | solution.py:373
  48.0 1.6 %copy.7 = f32[2,128,128]{2,1,0:T(8,128)} copy(f32[2,128,128]{2,1,0:T(8,128)} %exchange.1) | data formatting | bytes 262144

commit v6 on v4

--- a/solution.py
+++ b/solution.py
@@ -22,7 +22,7 @@
 DEPTH = SPAN * MSG
 ORDER = ((2, 2), (1, 2), (2, 1), (2, 3), (3, 2), (0, 2), (1, 1), (1, 3),
          (2, 0), (3, 1), (3, 3), (0, 1), (0, 3), (1, 0), (3, 0))
-TURNS = (2, 1, 3, 0)
+TURNS = (1, 2, 3, 0)
 
 
 def dot(a, b, dims=((1,), (0,))):

time: 49.5 us -> 49.5 us (level)
  no operation moved by 1% of the time
where the time goes in v6:
time: 49.5 us; the launch traced here: 49.4 us
  Pallas kernels  47.8 us (97%)
  local copies, waits for them, and re-layouts  1.57 us (3%)
    pallas_call x1, Pallas kernels, local(): pl.pallas_call(kernel, out_shape=jax.ShapeDtypeStruct(trials.shape, f32),...  47.8 us
    unnamed x1, local copies, waits for them, and re-layouts  1.57 us

profile of v6, /device:TPU:1, one launch (start us, length us, event | category | flops | bytes accessed | tf_op | source)
XLA Modules:
  0.0 49.4 jit_solution(9576081165216056020)
XLA Ops:
  0.0 47.8 %exchange.1 = f32[2,128,128]{2,1,0:T(8,128)} custom-call(bf16[2,2048,128]{2,1,0:T(8,128)(2,1)} %bitcast.3, bf16[2,128,128]{2,1,0:T(8,128)(2,1)} %v_hbm.1, s32[2,64]{1,0:T(2,128)} %bitcast.4, s32[1,256]{1,0:T(1,128)} %bitcast.5, s32[256,128]{1,0:T(8,128)} %dom_hbm.1), custom_call_target="tpu_custom_call" | custom-call | tf_op jit(solution)/shard_map/exchange/pallas_call | solution.py:372
  47.9 1.6 %copy.7 = f32[2,128,128]{2,1,0:T(8,128)} copy(f32[2,128,128]{2,1,0:T(8,128)} %exchange.1) | data formatting | bytes 262144
